TPU v7x, 32 devices: a whole 2x2x4 slice. The times are simulated.
32 devices in a mesh: dir: 2 (over x), dp: 16 (over z, y, core).
Axes of the slice: x: 2, y: 2, z: 4, core: 2. Of those that a mesh axis runs over, the one named last changes fastest.
Arguments:
- resid_in: bfloat16 [2, 4096, 768], P(None, 'dp'), may hold values from -6 to 6
- grad_out: bfloat16 [2, 4096, 768], P(None, 'dp'), may hold values from -6 to 6
- seq_spans: int32 [2, 32], P(None, 'dp'), may hold values from 0 to 2, as said below
- in_gain: bfloat16 [2, 768], P(None, 'dp'), may hold values from 0.099609375 to 1.8984375
- w_gate_in: bfloat16 [2, 768, 1536], P(None, 'dp'), may hold values from -0.21875 to 0.21875
- w_conv_in: bfloat16 [2, 768, 1792], P(None, 'dp'), may hold values from -0.21875 to 0.21875
- w_step: bfloat16 [2, 768, 48], P(None, 'dp'), may hold values from -0.21875 to 0.21875
- conv_weight: bfloat16 [2, 4, 1792], P(None, None, 'dp'), may hold values from -3 to 3
- conv_bias: bfloat16 [2, 1792], P(None, 'dp'), may hold values from -3 to 3
- step_bias: float32 [2, 48], replicated, may hold values from -6 to -1
- decay_log: float32 [2, 24], replicated, may hold values from -1 to 1.5
- skip_gain: float32 [2, 24], replicated, may hold values from 0.5 to 1.5
- out_gain: bfloat16 [2, 1536], P(None, 'dp'), may hold values from 0.099609375 to 1.8984375
- w_out: bfloat16 [2, 1536, 768], P(None, 'dp'), may hold values from -0.15625 to 0.15625
Outputs:
- resid_out: bfloat16 [2, 4096, 768], P(None, 'dp')
- grad_in: float32 [2, 4096, 768], P(None, 'dp')
- grad_in_gain: float32 [2, 768], P(None, 'dp')
- grad_gate_in: float32 [2, 768, 1536], P(None, 'dp')
- grad_conv_in: float32 [2, 768, 1792], P(None, 'dp')
- grad_step: float32 [2, 768, 48], P(None, 'dp')
- grad_conv_weight: float32 [2, 4, 1792], P(None, None, 'dp')
- grad_conv_bias: float32 [2, 1792], P(None, 'dp')
- grad_step_bias: float32 [2, 48], replicated
- grad_decay_log: float32 [2, 24], replicated
- grad_skip_gain: float32 [2, 24], replicated
- grad_out_gain: float32 [2, 1536], P(None, 'dp')
- grad_w_out: float32 [2, 1536, 768], P(None, 'dp')
Inputs may be any that keep to these rules, and one draw needn't show every extreme that they name: `seq_spans`: A run's 2 entries are 0, 1 or 2, nonzero ones first, summing to 1 or more and 2 at most; in each micro-batch some run holds one sequence of 2 blocks.
All inputs are finite; a program needn't handle non-finite values.
Results may differ from a plain program's by a relative error of at most 0.012.
Values may be sent and summed in bfloat16 or wider, within the bound.
A program may use at most 384 MiB of HBM per device.

v0:
```python
import jax
import jax.numpy as jnp
from jax import lax
from jax.sharding import PartitionSpec as P

H = 24
P_SIZE = 64
N = 64
K = 4
BLOCK = 128


def partner(block, axis, distance):
    count = lax.axis_size(axis)
    route = []
    for low in range(count):
        high = low | 1 << distance
        if high != low and high < count:
            route += [(low, high), (high, low)]
    return lax.ppermute(block, axis, route)


def seq_markers(lengths, nblocks):
    ends_cum = jnp.cumsum(lengths)
    begins = ends_cum - lengths
    filled = ends_cum[-1]
    block_ids = jnp.arange(nblocks, dtype=jnp.int32)
    block_open = jnp.any(
        (begins[None, :] == block_ids[:, None]) & (lengths[None, :] > 0), axis=1
    ) | (block_ids >= filled)
    block_close = jnp.concatenate([block_open[1:], jnp.ones((1,), bool)])
    offset = jnp.arange(BLOCK, dtype=jnp.int32)
    tok_first = (block_open[:, None] & (offset[None, :] == 0)).reshape(-1)
    tok_last = (block_close[:, None] & (offset[None, :] == BLOCK - 1)).reshape(-1)
    tok_live = jnp.repeat(block_ids < filled, BLOCK)
    open_tok = jnp.repeat(block_open, BLOCK)
    return tuple(
        (
            flag.astype(jnp.float32)
            for flag in (block_open, block_close, tok_first, tok_last, tok_live, open_tok)
        )
    )


def in_norm(residual, gain_vec):
    return (
        residual
        * lax.rsqrt(jnp.mean(residual * residual, axis=-1, keepdims=True) + 1e-05)
        * gain_vec[None, :]
    )


def conv_act(conv_in, conv_taps, conv_shift, markers):
    open_tok = markers[5]
    offset = jnp.arange(conv_in.shape[0], dtype=jnp.int32) % BLOCK
    summed = conv_shift[None, :] + conv_taps[0][None, :] * conv_in
    for lag_step in range(1, K):
        lagged = jnp.concatenate(
            [jnp.zeros((lag_step, conv_in.shape[1]), conv_in.dtype), conv_in[:-lag_step]], 0
        )
        lag_keep = 1.0 - open_tok * (offset < lag_step).astype(open_tok.dtype)
        summed = summed + conv_taps[lag_step][None, :] * lagged * lag_keep[:, None]
    return jax.nn.silu(summed)


def block_scan(values_in, b_proj, c_proj, step_size, log_decay, block_open):
    nblocks = block_open.shape[0]
    heads_q = values_in.reshape(nblocks, BLOCK, H, P_SIZE)
    keys_q = b_proj.reshape(nblocks, BLOCK, N)
    query_q = c_proj.reshape(nblocks, BLOCK, N)
    steps_q = step_size.reshape(nblocks, BLOCK, H).transpose(0, 2, 1)
    cumulative = jnp.cumsum(log_decay.reshape(nblocks, BLOCK, H).transpose(0, 2, 1), axis=2)
    log_gap = cumulative[:, :, :, None] - cumulative[:, :, None, :]
    causal = (
        jnp.arange(BLOCK, dtype=jnp.int32)[:, None] >= jnp.arange(BLOCK, dtype=jnp.int32)[None, :]
    )
    decays = jnp.where(causal[None, None], jnp.exp(jnp.minimum(log_gap, 0.0)), 0.0)
    scores = jnp.einsum("cin,cjn->cij", query_q, keys_q, precision=lax.Precision.HIGHEST)
    mixing = decays * scores[:, None, :, :] * steps_q[:, :, None, :]
    within = jnp.einsum("chij,cjhp->cihp", mixing, heads_q, precision=lax.Precision.HIGHEST)
    to_end = jnp.exp(cumulative[:, :, -1:] - cumulative) * steps_q
    weighted = heads_q * to_end.transpose(0, 2, 1)[..., None]
    states = jnp.einsum("cjhp,cjn->chpn", weighted, keys_q, precision=lax.Precision.HIGHEST)
    through = jnp.exp(cumulative[:, :, -1])
    keeping = 1.0 - block_open

    def advance(carried, element):
        state_here, decay_here, keep_here = element
        entering = carried * keep_here
        return (entering * decay_here[:, None, None] + state_here, entering)

    _, entering = lax.scan(
        advance, jnp.zeros((H, P_SIZE, N), states.dtype), (states, through, keeping)
    )
    carried_in = jnp.einsum("cin,chpn->cihp", query_q, entering, precision=lax.Precision.HIGHEST)
    carried_in = carried_in * jnp.exp(cumulative).transpose(0, 2, 1)[..., None]
    return (within + carried_in).reshape(nblocks * BLOCK, H * P_SIZE)


def scan_dir(values_in, b_proj, c_proj, step_raw, bias_half, decay_log, block_open, tok_first):
    step_size = jax.nn.softplus(step_raw + bias_half[None, :])
    log_decay = -step_size * jnp.exp(decay_log)[None, :]
    scanned = block_scan(values_in, b_proj, c_proj, step_size, log_decay, block_open)
    shifted = jnp.concatenate([jnp.zeros((1, scanned.shape[1]), scanned.dtype), scanned[:-1]], 0)
    return shifted * (1.0 - tok_first)[:, None]


def direction(conv_out, step_raw, bias_all, decay_log, markers, which_way):
    block_open, block_close, tok_first, tok_last = markers[:4]
    inner_width = H * P_SIZE
    offset_col = inner_width + 2 * N * which_way
    values_in = conv_out[:, :inner_width]
    b_proj = conv_out[:, offset_col : offset_col + N]
    c_proj = conv_out[:, offset_col + N : offset_col + 2 * N]
    step_half = step_raw[:, H * which_way : H * which_way + H]
    bias_half = bias_all[H * which_way : H * which_way + H]
    if which_way == 0:
        return scan_dir(
            values_in, b_proj, c_proj, step_half, bias_half, decay_log, block_open, tok_first
        )
    reversed_out = scan_dir(
        jnp.flip(values_in, 0),
        jnp.flip(b_proj, 0),
        jnp.flip(c_proj, 0),
        jnp.flip(step_half, 0),
        bias_half,
        decay_log,
        jnp.flip(block_close, 0),
        jnp.flip(tok_last, 0),
    )
    return jnp.flip(reversed_out, 0)


def own_way(conv_out, step_raw, bias_all, decay_log, markers, group):
    return lax.cond(
        group == 0,
        lambda operands: direction(operands[0], operands[1], operands[2], operands[3], markers, 0),
        lambda operands: direction(operands[0], operands[1], operands[2], operands[3], markers, 1),
        (conv_out, step_raw, bias_all, decay_log),
    )


def post_mix(summed_y, conv_out, skip_vec, gate_pre, gain_vec):
    values_in = conv_out[:, : H * P_SIZE]
    mixed = summed_y + (values_in.reshape(-1, H, P_SIZE) * skip_vec[None, :, None]).reshape(
        -1, H * P_SIZE
    )
    gated = mixed * jax.nn.silu(gate_pre)
    scale = lax.rsqrt(jnp.mean(gated * gated, axis=-1, keepdims=True) + 1e-05)
    return gated * scale * gain_vec[None, :]


def fetch_layer(
    in_gain, w_gate_in, w_conv_in, w_step, conv_weight, conv_bias, out_gain, w_out, layer_idx
):
    return (
        lax.all_gather(in_gain[layer_idx], "dp", axis=0, tiled=True),
        lax.all_gather(w_gate_in[layer_idx], "dp", axis=0, tiled=True),
        lax.all_gather(w_conv_in[layer_idx], "dp", axis=0, tiled=True),
        lax.all_gather(w_step[layer_idx], "dp", axis=0, tiled=True),
        lax.all_gather(conv_weight[layer_idx], "dp", axis=1, tiled=True),
        lax.all_gather(conv_bias[layer_idx], "dp", axis=0, tiled=True),
        lax.all_gather(out_gain[layer_idx], "dp", axis=0, tiled=True),
        lax.all_gather(w_out[layer_idx], "dp", axis=0, tiled=True),
    )


def fetch_again(
    in_gain, w_gate_in, w_conv_in, w_step, conv_weight, conv_bias, out_gain, w_out, layer_idx
):
    return (
        lax.all_gather(in_gain[layer_idx], "dp", axis=0, tiled=True),
        lax.all_gather(w_gate_in[layer_idx], "dp", axis=0, tiled=True),
        lax.all_gather(w_conv_in[layer_idx], "dp", axis=0, tiled=True),
        lax.all_gather(w_step[layer_idx], "dp", axis=0, tiled=True),
        lax.all_gather(conv_weight[layer_idx], "dp", axis=1, tiled=True),
        lax.all_gather(conv_bias[layer_idx], "dp", axis=0, tiled=True),
        lax.all_gather(out_gain[layer_idx], "dp", axis=0, tiled=True),
        lax.all_gather(w_out[layer_idx], "dp", axis=0, tiled=True),
    )


def scatter_grads(totals):
    return (
        lax.psum_scatter(totals[0], "dp", scatter_dimension=1, tiled=True),
        lax.psum_scatter(totals[1], "dp", scatter_dimension=1, tiled=True),
        lax.psum_scatter(totals[2], "dp", scatter_dimension=1, tiled=True),
        lax.psum_scatter(totals[3], "dp", scatter_dimension=1, tiled=True),
        lax.psum_scatter(totals[4], "dp", scatter_dimension=2, tiled=True),
        lax.psum_scatter(totals[5], "dp", scatter_dimension=1, tiled=True),
        lax.psum_scatter(totals[6], "dp", scatter_dimension=1, tiled=True),
        lax.psum_scatter(totals[7], "dp", scatter_dimension=1, tiled=True),
    )


def add_up(earlier, current):
    if earlier is None:
        return current
    return tuple((first_term + second_term for first_term, second_term in zip(earlier, current)))


def contract_rows(left_in, right_in):
    return lax.dot_general(
        left_in, right_in, (((0,), (0,)), ((), ())), preferred_element_type=jnp.float32
    )


def contract_cols(left_in, right_in):
    return lax.dot_general(
        left_in, right_in, (((1,), (1,)), ((), ())), preferred_element_type=jnp.float32
    )


def shards(
    resid_in,
    grad_out,
    seq_spans,
    in_gain,
    w_gate_in,
    w_conv_in,
    w_step,
    conv_weight,
    conv_bias,
    step_bias,
    decay_log,
    skip_gain,
    out_gain,
    w_out,
):
    layer_count = in_gain.shape[0]
    micro_count = resid_in.shape[0]
    nblocks = resid_in.shape[1] // BLOCK
    group = lax.axis_index("dir")
    weight_totals = None
    head_totals = None
    outputs_res = []
    outputs_grad = []
    for micro_idx in range(micro_count):
        markers = seq_markers(seq_spans[micro_idx], nblocks)
        tok_live = markers[4]
        residual = resid_in[micro_idx].astype(jnp.float32)
        saved = []
        for layer_idx in range(layer_count):
            weights_now = fetch_layer(
                in_gain,
                w_gate_in,
                w_conv_in,
                w_step,
                conv_weight,
                conv_bias,
                out_gain,
                w_out,
                layer_idx,
            )
            gain_in, gate_full, conv_full, step_full, taps_full, shift_full, gain_out, out_full = (
                weights_now
            )
            normed = in_norm(residual, gain_in.astype(jnp.float32)).astype(jnp.bfloat16)
            gate_pre = jnp.dot(normed, gate_full, preferred_element_type=jnp.float32)
            conv_in = jnp.dot(normed, conv_full, preferred_element_type=jnp.float32)
            step_raw = jnp.dot(normed, step_full, preferred_element_type=jnp.float32)
            conv_out = conv_act(
                conv_in, taps_full.astype(jnp.float32), shift_full.astype(jnp.float32), markers
            )
            own_y = own_way(
                conv_out, step_raw, step_bias[layer_idx], decay_log[layer_idx], markers, group
            )
            other_y = partner(own_y, "dir", 0)
            summed_y = own_y + other_y
            normed_out = post_mix(
                summed_y, conv_out, skip_gain[layer_idx], gate_pre, gain_out.astype(jnp.float32)
            ).astype(jnp.bfloat16)
            branch = jnp.dot(normed_out, out_full, preferred_element_type=jnp.float32)
            saved.append((residual, normed, gate_pre, conv_in, step_raw, summed_y))
            residual = residual + tok_live[:, None] * branch
        outputs_res.append(residual.astype(jnp.bfloat16))
        grad_res = grad_out[micro_idx].astype(jnp.float32)
        layer_grads = [None] * layer_count
        layer_heads = [None] * layer_count
        for layer_idx in reversed(range(layer_count)):
            weights_now = fetch_again(
                in_gain,
                w_gate_in,
                w_conv_in,
                w_step,
                conv_weight,
                conv_bias,
                out_gain,
                w_out,
                layer_idx,
            )
            gain_in, gate_full, conv_full, step_full, taps_full, shift_full, gain_out, out_full = (
                weights_now
            )
            res_in, normed, gate_pre, conv_in, step_raw, summed_y = saved[layer_idx]
            gain_in_f = gain_in.astype(jnp.float32)
            gain_out_f = gain_out.astype(jnp.float32)
            grad_branch = (tok_live[:, None] * grad_res).astype(jnp.bfloat16)
            conv_out, conv_pull = jax.vjp(
                lambda source, taps, shift: conv_act(source, taps, shift, markers),
                conv_in,
                taps_full.astype(jnp.float32),
                shift_full.astype(jnp.float32),
            )
            normed_pre, post_pull = jax.vjp(
                post_mix, summed_y, conv_out, skip_gain[layer_idx], gate_pre, gain_out_f
            )
            normed_out = normed_pre.astype(jnp.bfloat16)
            grad_wout = contract_rows(normed_out, grad_branch)
            grad_normed_out = contract_cols(grad_branch, out_full)
            grad_y, grad_conv_post, grad_skip, grad_gate, grad_gain_out = post_pull(grad_normed_out)
            _, scan_pull = jax.vjp(
                lambda source, steps, biases, decays: own_way(
                    source, steps, biases, decays, markers, group
                ),
                conv_out,
                step_raw,
                step_bias[layer_idx],
                decay_log[layer_idx],
            )
            part_conv, part_step, part_bias, part_decay = scan_pull(grad_y)
            grad_conv_scan, grad_step_raw, grad_bias, grad_decay = lax.psum(
                (part_conv, part_step, part_bias, part_decay), "dir"
            )
            grad_conv_out = grad_conv_post + grad_conv_scan
            grad_conv_in, grad_taps, grad_shift = conv_pull(grad_conv_out)
            gate_low = grad_gate.astype(jnp.bfloat16)
            conv_low = grad_conv_in.astype(jnp.bfloat16)
            step_low = grad_step_raw.astype(jnp.bfloat16)
            grad_wgate = contract_rows(normed, gate_low)
            grad_wconv = contract_rows(normed, conv_low)
            grad_wstep = contract_rows(normed, step_low)
            grad_normed = (
                contract_cols(gate_low, gate_full)
                + contract_cols(conv_low, conv_full)
                + contract_cols(step_low, step_full)
            )
            _, norm_pull = jax.vjp(in_norm, res_in, gain_in_f)
            grad_res_norm, grad_gain_in = norm_pull(grad_normed)
            grad_res = grad_res + grad_res_norm
            layer_grads[layer_idx] = (
                grad_gain_in,
                grad_wgate,
                grad_wconv,
                grad_wstep,
                grad_taps,
                grad_shift,
                grad_gain_out,
                grad_wout,
            )
            layer_heads[layer_idx] = (grad_bias, grad_decay, grad_skip)
        outputs_grad.append(grad_res)
        stacked = tuple(
            (
                jnp.stack([layer_grads[layer_idx][member] for layer_idx in range(layer_count)])
                for member in range(8)
            )
        )
        heads_stacked = tuple(
            (
                jnp.stack([layer_heads[layer_idx][member] for layer_idx in range(layer_count)])
                for member in range(3)
            )
        )
        head_totals = add_up(head_totals, heads_stacked)
        weight_totals = add_up(weight_totals, scatter_grads(stacked))
    grad_bias_all, grad_decay_all, grad_skip_all = lax.psum(
        (head_totals[0], head_totals[1], head_totals[2]), "dp"
    )
    return (
        jnp.stack(outputs_res),
        jnp.stack(outputs_grad),
        weight_totals[0],
        weight_totals[1],
        weight_totals[2],
        weight_totals[3],
        weight_totals[4],
        weight_totals[5],
        grad_bias_all,
        grad_decay_all,
        grad_skip_all,
        weight_totals[6],
        weight_totals[7],
    )


def solution(mesh):
    placed = (
        P(None, "dp", None),
        P(None, "dp", None),
        P(None, "dp"),
        P(None, "dp"),
        P(None, "dp", None),
        P(None, "dp", None),
        P(None, "dp", None),
        P(None, None, "dp"),
        P(None, "dp"),
        P(),
        P(),
        P(),
        P(None, "dp"),
        P(None, "dp", None),
    )
    return jax.shard_map(
        shards,
        mesh=mesh,
        in_specs=placed,
        out_specs=(
            P(None, "dp", None),
            P(None, "dp", None),
            P(None, "dp"),
            P(None, "dp", None),
            P(None, "dp", None),
            P(None, "dp", None),
            P(None, None, "dp"),
            P(None, "dp"),
            P(),
            P(),
            P(),
            P(None, "dp"),
            P(None, "dp", None),
        ),
        check_vma=False,
    )
```

profile of v0, /device:TPU:0, one launch (start us, length us, event | category | flops | bytes accessed | tf_op | source)
XLA Modules:
  0.0 2207.1 jit_solution(1241674826475841340)
XLA Ops:
  25.9 63.5 %all-reduce.127 = (bf16[768]{0:T(1024)(128)(2,1)S(1)}, bf16[1792]{0:T(1024)(128)(2,1)S(1)}, bf16[1536]{0:T(1024)(128)(2,1)}, bf16[768]{0:T(1024)(128)(2,1)}, bf1...) all-reduce(bf16[768]{0:T(1024)(128)(2,1)S(1)} %dynamic-update-slice, ...), channel_id=2, replica_groups=mesh['dir'=2,'dp'=16] {'dp'}, use_global_device_ids=true, to_apply=%add.116 | all-reduce | flops 8192 | bytes 32768
  90.5 22.5 %all-gather.3 = bf16[1,4,1792]{1,0,2:T(2,128)(2,1)S(1)} all-gather(bf16[1,4,112]{1,0,2:T(2,128)(2,1)S(1)} %copy.1733), channel_id=5, replica_groups=mesh['dir'=2,'dp'=16] {'dp'}, dimensions={2}, use_global_device_ids=true | all-gather | bytes 15232 | tf_op jit(solution)/shard_map/all_gather | solution.py:161
  114.1 37.1 %slice_reduce_fusion.23 = (f32[1792]{0:T(1024)S(1)}, f32[1792]{0:T(1024)S(1)}, f32[1792]{0:T(1024)S(1)}, f32[1792]{0:T(1024)S(1)}) fusion(f32[1,4,1792]{1,0,2:T(1,128)S(1)} %convert_element_type.347), kind=kLoop, calls=%fused_computation.1451 | loop fusion | bytes 57344 | tf_op jit(solution)/shard_map/slice | solution.py:56
  151.9 18.9 all-gather.1
  179.0 5.0 fusion.763
  184.1 48.7 %conditional.14 = (f32[256,1536]{1,0:T(8,128)}) conditional(s32[]{:T(128)} %convert_element_type.280, (f32[256,48]{0,1:T(8,128)S(1)}, f32[48]{0:T(128)S(1)}, f32[24]{0:T(128)S(1)}, f32[256,1792]{1,0:T(8,128)}, f32[2]{0:T(128)}, /*index=5*/f32[256]{0:T(256)}) %tuple.474, (f32[256,48]{0,1:T(8,128)S(1)}, f32[48]{0:T(128)S(1)}, f32[24]{0:T(128)S(1)}, ...), branch_computations={%region_25.29_spmd, %region_29.33_spmd} | conditional | flops 1240084736 | bytes 49698944 | solution.py:135
  203.0 9.0 while.354
  213.4 9.1 fusion.525
  232.8 40.3 %collective-permute-start.2 = (f32[256,1536]{1,0:T(8,128)}, f32[256,1536]{1,0:T(8,128)}, u32[]{:S(2)}, u32[]{:S(2)}) collective-permute-start(f32[256,1536]{1,0:T(8,128)} %get-tuple-element.5340), channel_id=1, source_target_pairs={{0,16},{16,0},{1,17},{17,1},{2,18},{18,2},{3,19},{19,3},{4,20},{20... | collective-permute-start | bytes 4718600 | tf_op jit(solution)/shard_map/ppermute | solution.py:20
  273.1 52.2 %conditional.12 = (f32[256,1536]{1,0:T(8,128)}) conditional(s32[]{:T(128)} %convert_element_type.280, (f32[256,48]{0,1:T(8,128)}, f32[48]{0:T(128)}, f32[24]{0:T(128)}, f32[256,1792]{1,0:T(8,128)S(1)}, f32[2]{0:T(128)}, /*index=5*/f32[256]{0:T(256)}) %tuple.1322, (f32[256,48]{0,1:T(8,128)}, f32[48]{0:T(128)}, f32[24]{0:T(128)}, ...), branch_computations={%region_3.7_spmd, %region_7.11_spmd} | conditional | flops 1240084736 | bytes 49698944 | solution.py:135
  295.3 9.3 while.352
  305.9 9.1 fusion.425
  325.3 42.3 %collective-permute-start = (f32[256,1536]{1,0:T(8,128)}, f32[256,1536]{1,0:T(8,128)}, u32[]{:S(2)}, u32[]{:S(2)}) collective-permute-start(f32[256,1536]{1,0:T(8,128)} %get-tuple-element.5338), channel_id=1, source_target_pairs={{0,16},{16,0},{1,17},{17,1},{2,18},{18,2},{3,19},{19,3},{4,20},{20... | collective-permute-start | bytes 4718600 | tf_op jit(solution)/shard_map/ppermute | solution.py:20
  372.0 20.7 all-gather.11
  393.7 18.7 all-gather.9
  413.8 37.1 %slice_reduce_fusion.19 = (f32[1792]{0:T(1024)S(1)}, f32[1792]{0:T(1024)S(1)}, f32[1792]{0:T(1024)S(1)}, f32[1792]{0:T(1024)S(1)}) fusion(f32[1,4,1792]{1,0,2:T(1,128)S(1)} %convert_element_type.351), kind=kLoop, calls=%fused_computation.1447 | loop fusion | bytes 57344 | tf_op jit(solution)/shard_map/slice | solution.py:56
  453.9 6.5 multiply_reduce_fusion.47
  470.1 5.1 fusion.762
  475.2 41.1 %conditional.13 = (f32[256,1536]{1,0:T(8,128)}) conditional(s32[]{:T(128)} %convert_element_type.280, (f32[256,48]{0,1:T(8,128)S(1)}, f32[48]{0:T(128)S(1)}, f32[24]{0:T(128)S(1)}, f32[256,1792]{1,0:T(8,128)}, f32[2]{0:T(128)}, /*index=5*/f32[256]{0:T(256)S(1)}) %tuple.1328, (f32[256,48]{0,1:T(8,128)S(1)}, f32[48]{0:T(128)S(1)}, f32[24]{0:T(128)S(1)}, ...), branch_computations={%region_13.17_spmd, %region_17.21_spmd} | conditional | flops 1240084736 | bytes 65358088 | solution.py:135
  489.8 8.9 while.353
  500.8 8.0 fusion.475
  516.3 33.1 %collective-permute-start.1 = (f32[256,1536]{1,0:T(8,128)}, f32[256,1536]{1,0:T(8,128)}, u32[]{:S(2)}, u32[]{:S(2)}) collective-permute-start(f32[256,1536]{1,0:T(8,128)} %get-tuple-element.5339), channel_id=1, source_target_pairs={{0,16},{16,0},{1,17},{17,1},{2,18},{18,2},{3,19},{19,3},{4,20},{20... | collective-permute-start | bytes 4718600 | tf_op jit(solution)/shard_map/ppermute | solution.py:20
  550.9 53.6 %conditional.16 = (f32[256,24]{0,1:T(8,128)}, f32[24]{0:T(128)}, f32[1,24]{1,0:T(1,128)S(1)}, f32[256,24]{0,1:T(8,128)}, f32[2,24,128,128]{3,2,1,0:T(8,128)}, /*...) conditional(s32[]{:T(128)} %convert_element_type.280, ...), branch_computations={%region_45.50_spmd, %region_49.54_spmd} | conditional | flops 638107904 | bytes 62380248 | solution.py:135
  571.5 14.5 while.364
  592.9 7.6 broadcast_multiply_fusion.19
  606.5 70.0 %conditional.20 = (f32[256,24]{0,1:T(8,128)}, f32[24]{0:T(128)}, f32[1,24]{1,0:T(1,128)}, f32[256,24]{0,1:T(8,128)}, f32[2,24,128,128]{3,2,1,0:T(8,128)}, /*inde...) conditional(s32[]{:T(128)} %convert_element_type.280, ...), branch_computations={%region_125.130_spmd, %region_129.134_spmd} | conditional | flops 638107904 | bytes 46452956 | solution.py:135
  642.8 13.5 while.366
  664.6 7.5 broadcast_multiply_fusion.31
  677.1 65.4 %conditional.15 = (f32[256,1536]{1,0:T(8,128)}) conditional(s32[]{:T(128)} %convert_element_type.280, (f32[256,48]{0,1:T(8,128)}, f32[48]{0:T(128)}, f32[24]{0:T(128)}, f32[256,1792]{1,0:T(8,128)S(1)}, f32[2]{0:T(128)}, /*index=5*/f32[256]{0:T(256)}) %tuple.1270, (f32[256,48]{0,1:T(8,128)}, f32[48]{0:T(128)}, f32[24]{0:T(128)}, ...), branch_computations={%region_35.39_spmd, %region_39.43_spmd} | conditional | flops 1240084736 | bytes 49794684 | solution.py:135
  703.5 13.3 while.355
  720.9 9.2 fusion.575
  742.5 72.7 %collective-permute-start.3 = (f32[256,1536]{1,0:T(8,128)}, f32[256,1536]{1,0:T(8,128)}, u32[]{:S(2)}, u32[]{:S(2)}) collective-permute-start(f32[256,1536]{1,0:T(8,128)} %get-tuple-element.5341), channel_id=1, source_target_pairs={{0,16},{16,0},{1,17},{17,1},{2,18},{18,2},{3,19},{19,3},{4,20},{20... | collective-permute-start | bytes 4718600 | tf_op jit(solution)/shard_map/ppermute | solution.py:20
  815.2 6.3 multiply_reduce_fusion.46
  831.6 18.8 collective-permute-done.3
  859.8 78.7 %conditional.17 = (f32[256,1792]{0,1:T(8,128)}, f32[256,48]{0,1:T(8,128)}, f32[48]{0:T(128)}, f32[24]{0:T(128)S(1)}) conditional(s32[]{:T(128)} %convert_element_type.280, (f32[256,1536]{1,0:T(8,128)}, f32[256,1]{0,1:T(1,128)S(1)}, f32[2,128,24,1]{1,2,0,3:T(8,128)}, f32[2,24,64,64]{3,2,1,0:T(8,128)S(1)}, f32[2,128,24,64]{1,0,3,2:T(2,128)}, ...), branch_computations={%region_53.68_spmd, %region_67.82_spmd} | conditional | flops 2480536064 | bytes 142671008 | solution.py:135
  883.3 10.5 while.357
  899.4 10.7 multiply_reduce_fusion.2
  941.3 76.2 %conditional.21 = (f32[256,1792]{0,1:T(8,128)}, f32[256,48]{0,1:T(8,128)}, f32[48]{0:T(128)S(1)}, f32[24]{0:T(128)S(1)}) conditional(s32[]{:T(128)} %convert_element_type.280, (f32[256,1536]{1,0:T(8,128)}, f32[256,1]{0,1:T(1,128)S(1)}, f32[2,128,24,1]{1,2,0,3:T(8,128)}, f32[2,24,64,64]{3,2,1,0:T(8,128)}, f32[2,128,24,64]{1,0,3,2:T(2,128)}, ...), branch_computations={%region_133.148_spmd, %region_147.162_spmd} | conditional | flops 2480536064 | bytes 154662592 | solution.py:135
  967.0 9.4 while.361
  980.7 10.0 multiply_reduce_fusion.10
  1022.6 34.2 %conditional.18 = (f32[256,24]{0,1:T(8,128)}, f32[24]{0:T(128)}, f32[1,24]{1,0:T(1,128)S(1)}, f32[256,24]{0,1:T(8,128)}, f32[2,24,128,128]{3,2,1,0:T(8,128)}, /*...) conditional(s32[]{:T(128)} %convert_element_type.280, ...), branch_computations={%region_85.90_spmd, %region_89.94_spmd} | conditional | flops 638107904 | bytes 72328944 | solution.py:135
  1034.5 7.1 while.365
  1045.8 7.7 broadcast_multiply_fusion.25
  1058.1 51.6 %conditional.22 = (f32[256,24]{0,1:T(8,128)}, f32[24]{0:T(128)}, f32[1,24]{1,0:T(1,128)S(1)}, f32[256,24]{0,1:T(8,128)S(1)}, f32[2,24,128,128]{3,2,1,0:T(8,128)}...) conditional(s32[]{:T(128)} %convert_element_type.280, ...), branch_computations={%region_165.170_spmd, %region_169.174_spmd} | conditional | flops 638107904 | bytes 57812500 | solution.py:135
  1081.6 11.1 while.367
  1098.7 7.6 broadcast_multiply_fusion.37
  1109.7 86.8 %all-reduce.124 = (bf16[256,48]{0,1:T(8,128)(2,1)S(1)}, bf16[256,48]{0,1:T(8,128)(2,1)S(1)}) all-reduce(f32[256,48]{0,1:T(8,128)} %get-tuple-element.3059, f32[256,48]{0,1:T(8,128)} %get-tuple-element.3001), channel_id=1, replica_groups=mesh['dir'=2,'dp'=16] {'dir'}, use_global_device_ids=true, to_apply=%region_162.164 | all-reduce | flops 24576 | bytes 147456 | tf_op jit(solution)/shard_map/psum | solution.py:322
  1237.7 80.1 %conditional.19 = (f32[256,1792]{0,1:T(8,128)}, f32[256,48]{0,1:T(8,128)}, f32[48]{0:T(128)}, f32[24]{0:T(128)}) conditional(s32[]{:T(128)} %convert_element_type.280, (f32[256,1536]{1,0:T(8,128)}, f32[256,1]{0,1:T(1,128)S(1)}, f32[2,128,24,1]{1,2,0,3:T(8,128)S(1)}, f32[2,24,64,64]{3,2,1,0:T(8,128)S(1)}, f32[2,128,24,64]{1,0,3,2:T(2,128)}, ...), branch_computations={%region_93.108_spmd, %region_107.122_spmd} | conditional | flops 2480536064 | bytes 142278240 | solution.py:135
  1264.3 8.0 while.359
  1277.8 10.1 multiply_reduce_fusion.6
  1320.6 76.9 %conditional.23 = (f32[256,1792]{0,1:T(8,128)}, f32[256,48]{0,1:T(8,128)}, f32[48]{0:T(128)}, f32[24]{0:T(128)}) conditional(s32[]{:T(128)} %convert_element_type.280, (f32[256,1536]{1,0:T(8,128)}, f32[256,1]{0,1:T(1,128)}, f32[2,128,24,1]{1,2,0,3:T(8,128)}, f32[2,24,64,64]{3,2,1,0:T(8,128)}, f32[2,128,24,64]{1,0,3,2:T(2,128)}, ...), branch_computations={%region_173.188_spmd, %region_187.202_spmd} | conditional | flops 2480536064 | bytes 154668320 | solution.py:135
  1346.1 8.0 while.363
  1359.1 10.0 multiply_reduce_fusion.14
  1410.4 60.5 %all-reduce.123 = (bf16[256,48]{0,1:T(8,128)(2,1)S(1)}, bf16[256,48]{0,1:T(8,128)(2,1)S(1)}, f32[1,48]{1,0:T(1,128)}, f32[1,48]{1,0:T(1,128)}, f32[1,48]{1,0:T(1...) all-reduce(f32[256,48]{0,1:T(8,128)S(1)} %copy-done.335, ...), channel_id=1, replica_groups=mesh['dir'=2,'dp'=16] {'dir'}, use_global_device_ids=true, to_apply=%region_202.204 | all-reduce | flops 24864 | bytes 149760 | tf_op jit(solution)/shard_map/psum | solution.py:322
  1495.0 50.4 %all-reduce.131.cloned.1.call-done = (f32[256,1792]{1,0:T(8,128)}, f32[256,1792]{1,0:T(8,128)}) async-done(((f32[256,1792]{1,0:T(8,128)}, f32[256,1792]{1,0:T(8,128)}), (f32[256,1792]{1,0:T(8,128)}, f32[256,1792]{1,0:T(8,128)})) %all-reduce.131.cloned.1.call-update) | async-done | bytes 3670032 | tf_op jit(solution)/shard_map/psum | solution.py:322
  1575.6 11.0 maximum_add_fusion.2
  1614.4 34.0 %all-reduce.122 = (f32[2,48]{1,0:T(2,128)}, f32[2,24]{1,0:T(2,128)}, f32[2,24]{1,0:T(2,128)}) all-reduce(f32[2,48]{1,0:T(2,128)S(1)} %maximum_add_fusion.8, f32[2,24]{1,0:T(2,128)S(1)} %maximum_add_fusion.9, f32[2,24]{1,0:T(2,128)S(1)} %maximum_add_fusion.10), channel_id=1, replica_groups=mesh['dir'=2,'dp'=16] {'dp'}, use_global_device_ids=true, to_apply=%region_244.246 | all-reduce | flops 192 | bytes 1536 | tf_op jit(solution)/shard_map/psum | solution.py:367
  1649.8 14.2 reduce-scatter.27.cloned.1.call-done
  1668.6 53.6 %reduce-scatter.25.cloned.1.call-done = f32[48,2]{1,0:T(8,128)} async-done(((f32[768,2]{1,0:T(8,128)}), f32[48,2]{1,0:T(8,128)}) %reduce-scatter.25.cloned.1.call-update) | async-done | bytes 400
  1723.5 58.5 %reduce-scatter.31.cloned.1.call-done = f32[112,2]{1,0:T(8,128)} async-done(((f32[1792,2]{1,0:T(8,128)}), f32[112,2]{1,0:T(8,128)}) %reduce-scatter.31.cloned.1.call-update) | async-done | bytes 912
  1783.5 58.1 %reduce-scatter.29.cloned.1.call-done = f32[112,8]{1,0:T(8,128)} async-done(((f32[1792,8]{1,0:T(8,128)}), f32[112,8]{1,0:T(8,128)}) %reduce-scatter.29.cloned.1.call-update) | async-done | bytes 3600
  1843.2 113.8 %reduce-scatter.23.cloned.1.call-done = f32[2,96,768]{2,1,0:T(8,128)} async-done(((f32[2,1536,768]{2,1,0:T(8,128)}), f32[2,96,768]{2,1,0:T(8,128)}) %reduce-scatter.23.cloned.1.call-update) | async-done | bytes 589840 | tf_op jit(solution)/shard_map/reduce_scatter | solution.py:192
  1957.0 115.7 %reduce-scatter.19.cloned.1.call-done = f32[2,48,1536]{2,1,0:T(8,128)} async-done(((f32[2,768,1536]{2,1,0:T(8,128)}), f32[2,48,1536]{2,1,0:T(8,128)}) %reduce-scatter.19.cloned.1.call-update) | async-done | bytes 589840 | tf_op jit(solution)/shard_map/reduce_scatter | solution.py:186
  2072.7 127.6 %reduce-scatter.21.cloned.1.call-done = f32[2,48,1792]{2,1,0:T(8,128)} async-done(((f32[2,768,1792]{2,1,0:T(8,128)}), f32[2,48,1792]{2,1,0:T(8,128)}) %reduce-scatter.21.cloned.1.call-update) | async-done | bytes 688144 | tf_op jit(solution)/shard_map/reduce_scatter | solution.py:187
  (1762 shorter events, 769.9 us)
Async XLA Ops:
  7.2 82.1 %copy-start.46 = (bf16[2,256,768]{2,1,0:T(8,128)(2,1)S(1)}, bf16[2,256,768]{2,1,0:T(8,128)(2,1)}, u32[]{:S(2)}) copy-start(bf16[2,256,768]{2,1,0:T(8,128)(2,1)} %param.87) | copy-start | bytes 2359300
  7.3 167.3 %all-gather.23.cloned.1.call-start = ((), (), s32[]{:S(2)}) async-start(), calls=%async_computation.8 | async-start | bytes 2924544 | tf_op jit(solution)/shard_map/all_gather | solution.py:159
  9.2 80.6 %copy-start.546 = (bf16[2,4,112]{2,1,0:T(4,128)(2,1)S(1)}, bf16[2,4,112]{2,1,0:T(4,128)(2,1)}, u32[]{:S(2)}) copy-start(bf16[2,4,112]{2,1,0:T(4,128)(2,1)} %param.94) | copy-start | bytes 5380
  9.3 441.7 %all-gather.25.cloned.1.call-start = ((), (), s32[]{:S(2)}) async-start(), calls=%async_computation.9 | async-start | bytes 2506752 | tf_op jit(solution)/shard_map/all_gather | solution.py:158
  11.0 449.5 %all-gather.27.cloned.1.call-start = ((), (), s32[]{:S(2)}) async-start(), calls=%async_computation.10 | async-start | bytes 2506752 | tf_op jit(solution)/shard_map/all_gather | solution.py:164
  11.9 453.9 %all-gather.29.cloned.1.call-start = ((), (), s32[]{:S(2)}) async-start(), calls=%async_computation.11 | async-start | bytes 2924544 | tf_op jit(solution)/shard_map/all_gather | solution.py:159
  12.4 802.8 %all-gather.31.cloned.1.call-start = ((), (), s32[]{:S(2)}) async-start(), calls=%async_computation.12 | async-start | bytes 2506752 | tf_op jit(solution)/shard_map/all_gather | solution.py:158
  13.0 809.7 %all-gather.33.cloned.1.call-start = ((), (), s32[]{:S(2)}) async-start(), calls=%async_computation.13 | async-start | bytes 2506752 | tf_op jit(solution)/shard_map/all_gather | solution.py:164
  13.6 1188.8 %all-reduce.133.cloned.1.call-start = ((), (), s32[]{:S(2)}) async-start(), calls=%async_computation.23 | async-start | bytes 7340032 | tf_op jit(solution)/shard_map/psum | solution.py:322
  16.1 96.9 %copy-start.550 = (f32[2]{0:T(128)}, f32[2]{0:T(128)S(1)}, u32[]{:S(2)}) copy-start(f32[2]{0:T(128)S(1)} %get-tuple-element.5929) | copy-start | bytes 28
  19.4 93.7 %copy-start.554 = (f32[2]{0:T(128)}, f32[2]{0:T(128)S(1)}, u32[]{:S(2)}) copy-start(f32[2]{0:T(128)S(1)} %get-tuple-element.5917) | copy-start | bytes 28
  89.4 364.3 %copy-start.215 = (f32[768]{0:T(1024)}, f32[768]{0:T(1024)S(1)}, u32[]{:S(2)}) copy-start(f32[768]{0:T(1024)S(1)} %convert_element_type.353) | copy-start | bytes 9220
  89.6 84.9 %copy-start.342 = (f32[256]{0:T(256)}, f32[256]{0:T(256)S(1)}, u32[]{:S(2)}) copy-start(f32[256]{0:T(256)S(1)} %fusion.902) | copy-start | bytes 3076
  89.7 361.3 %copy-start.333 = (f32[256]{0:T(256)}, f32[256]{0:T(256)S(1)}, u32[]{:S(2)}) copy-start(f32[256]{0:T(256)S(1)} %fusion.906) | copy-start | bytes 3076
  89.8 89.0 %copy-start.424 = (f32[256]{0:T(256)}, f32[256]{0:T(256)S(1)}, u32[]{:S(2)}) copy-start(f32[256]{0:T(256)S(1)} %get-tuple-element.6164) | copy-start | bytes 3076
  89.8 89.0 %copy-start.428 = (f32[256]{0:T(256)}, f32[256]{0:T(256)S(1)}, u32[]{:S(2)}) copy-start(f32[256]{0:T(256)S(1)} %get-tuple-element.6166) | copy-start | bytes 3076
  89.8 89.0 %copy-start.432 = (f32[256]{0:T(256)}, f32[256]{0:T(256)S(1)}, u32[]{:S(2)}) copy-start(f32[256]{0:T(256)S(1)} %get-tuple-element.6165) | copy-start | bytes 3076
  89.8 88.9 %copy-start.436 = (f32[256]{0:T(256)}, f32[256]{0:T(256)S(1)}, u32[]{:S(2)}) copy-start(f32[256]{0:T(256)S(1)} %get-tuple-element.6167) | copy-start | bytes 3076
  89.8 88.9 %copy-start.440 = (f32[256]{0:T(256)}, f32[256]{0:T(256)S(1)}, u32[]{:S(2)}) copy-start(f32[256]{0:T(256)S(1)} %get-tuple-element.6169) | copy-start | bytes 3076
  89.8 89.0 %copy-start.444 = (f32[256]{0:T(256)}, f32[256]{0:T(256)S(1)}, u32[]{:S(2)}) copy-start(f32[256]{0:T(256)S(1)} %get-tuple-element.6168) | copy-start | bytes 3076
  114.1 56.7 %copy-start.563 = (f32[2,24]{1,0:T(2,128)S(1)}, f32[2,24]{1,0:T(2,128)}, u32[]{:S(2)}) copy-start(f32[2,24]{1,0:T(2,128)} %param.97) | copy-start | bytes 580
  114.1 57.3 %copy-start.564 = (f32[2,48]{1,0:T(2,128)S(1)}, f32[2,48]{1,0:T(2,128)}, u32[]{:S(2)}) copy-start(f32[2,48]{1,0:T(2,128)} %param.96) | copy-start | bytes 1156
  184.1 269.7 %copy-start.26 = (f32[256,1792]{1,0:T(8,128)}, f32[256,1792]{1,0:T(8,128)S(1)}, u32[]{:S(2)}) copy-start(f32[256,1792]{1,0:T(8,128)S(1)} %get-tuple-element.5915) | copy-start | bytes 5505028
  232.8 220.9 %collective-permute-start.2 = (f32[256,1536]{1,0:T(8,128)}, f32[256,1536]{1,0:T(8,128)}, u32[]{:S(2)}, u32[]{:S(2)}) collective-permute-start(f32[256,1536]{1,0:T(8,128)} %get-tuple-element.5340), channel_id=1, source_target_pairs={{0,16},{16,0},{1,17},{17,1},{2,18},{18,2},{3,19},{19,3},{4,20},{20... | collective-permute-start | bytes 4718600 | tf_op jit(solution)/shard_map/ppermute | solution.py:20
  325.3 68.4 %copy-start.393 = (bf16[1,48,48]{2,1,0:T(8,128)(2,1)S(1)}, bf16[1,48,48]{2,1,0:T(8,128)(2,1)}, u32[]{:S(2)}) copy-start(bf16[1,48,48]{2,1,0:T(8,128)(2,1)} %get-tuple-element.6117) | copy-start | bytes 13828
  325.3 128.4 %collective-permute-start = (f32[256,1536]{1,0:T(8,128)}, f32[256,1536]{1,0:T(8,128)}, u32[]{:S(2)}, u32[]{:S(2)}) collective-permute-start(f32[256,1536]{1,0:T(8,128)} %get-tuple-element.5338), channel_id=1, source_target_pairs={{0,16},{16,0},{1,17},{17,1},{2,18},{18,2},{3,19},{19,3},{4,20},{20... | collective-permute-start | bytes 4718600 | tf_op jit(solution)/shard_map/ppermute | solution.py:20
  369.1 84.6 %copy-start.396 = (f32[1536]{0:T(1024)}, f32[1536]{0:T(1024)S(1)}, u32[]{:S(2)}) copy-start(f32[1536]{0:T(1024)S(1)} %mul.3631) | copy-start | bytes 18436
  369.8 94.0 %copy-start.331 = (f32[1536]{0:T(1024)}, f32[1536]{0:T(1024)S(1)}, u32[]{:S(2)}) copy-start(f32[1536]{0:T(1024)S(1)} %convert_element_type.355) | copy-start | bytes 18436
  370.5 94.4 %copy-start.389 = (f32[768]{0:T(1024)}, f32[768]{0:T(1024)S(1)}, u32[]{:S(2)}) copy-start(f32[768]{0:T(1024)S(1)} %convert_element_type.356) | copy-start | bytes 9220
  412.4 53.2 %copy-start.181 = (bf16[1,768,48]{2,1,0:T(8,128)(2,1)}, bf16[1,768,48]{2,1,0:T(8,128)(2,1)S(1)}, u32[]{:S(2)}) copy-start(bf16[1,768,48]{2,1,0:T(8,128)(2,1)S(1)} %all-gather.9) | copy-start | bytes 221188
  516.3 298.9 %collective-permute-start.1 = (f32[256,1536]{1,0:T(8,128)}, f32[256,1536]{1,0:T(8,128)}, u32[]{:S(2)}, u32[]{:S(2)}) collective-permute-start(f32[256,1536]{1,0:T(8,128)} %get-tuple-element.5339), channel_id=1, source_target_pairs={{0,16},{16,0},{1,17},{17,1},{2,18},{18,2},{3,19},{19,3},{4,20},{20... | collective-permute-start | bytes 4718600 | tf_op jit(solution)/shard_map/ppermute | solution.py:20
  550.2 300.2 %copy-start.368 = (f32[1536]{0:T(1024)}, f32[1536]{0:T(1024)S(1)}, u32[]{:S(2)}) copy-start(f32[1536]{0:T(1024)S(1)} %mul.3665) | copy-start | bytes 18436
  550.9 305.5 %copy-start.242 = (f32[1536]{0:T(1024)}, f32[1536]{0:T(1024)S(1)}, u32[]{:S(2)}) copy-start(f32[1536]{0:T(1024)S(1)} %convert_element_type.358) | copy-start | bytes 18436
  742.5 107.9 %collective-permute-start.3 = (f32[256,1536]{1,0:T(8,128)}, f32[256,1536]{1,0:T(8,128)}, u32[]{:S(2)}, u32[]{:S(2)}) collective-permute-start(f32[256,1536]{1,0:T(8,128)} %get-tuple-element.5341), channel_id=1, source_target_pairs={{0,16},{16,0},{1,17},{17,1},{2,18},{18,2},{3,19},{19,3},{4,20},{20... | collective-permute-start | bytes 4718600 | tf_op jit(solution)/shard_map/ppermute | solution.py:20
  859.8 78.7 %copy-start.202 = (f32[2,128,64]{1,0,2:T(2,128)S(1)}, f32[2,128,64]{1,0,2:T(2,128)}, u32[]{:S(2)}) copy-start(f32[2,128,64]{1,0,2:T(2,128)} %get-tuple-element.3038) | copy-start | bytes 196612
  859.8 78.7 %copy-start.228 = (f32[2,24,1,128]{3,0,1,2:T(2,128)S(1)}, f32[2,24,1,128]{3,0,1,2:T(2,128)}, u32[]{:S(2)}) copy-start(f32[2,24,1,128]{3,0,1,2:T(2,128)} %get-tuple-element.3035) | copy-start | bytes 73732
  859.8 78.8 %copy-start.504 = (f32[2,24]{1,0:T(2,128)S(1)}, f32[2,24]{1,0:T(2,128)}, u32[]{:S(2)}) copy-start(f32[2,24]{1,0:T(2,128)} %get-tuple-element.3048) | copy-start | bytes 580
  859.8 78.8 %copy-start.516 = (f32[256,1]{0,1:T(1,128)S(1)}, f32[256,1]{0,1:T(1,128)}, u32[]{:S(2)}) copy-start(f32[256,1]{0,1:T(1,128)} %copy-done.515) | copy-start | bytes 3076
  859.8 78.8 %copy-start.534 = (f32[24]{0:T(128)S(1)}, f32[24]{0:T(128)}, u32[]{:S(2)}) copy-start(f32[24]{0:T(128)} %get-tuple-element.3057) | copy-start | bytes 292
  1021.9 523.5 %all-reduce.131.cloned.1.call-start = ((), (), s32[]{:S(2)}) async-start(), calls=%async_computation.22 | async-start | bytes 7340032 | tf_op jit(solution)/shard_map/psum | solution.py:322
  1109.7 89.2 %copy-start.132 = (f32[2,128,24,64]{1,3,2,0:T(8,128)}, f32[2,128,24,64]{1,3,2,0:T(8,128)S(1)}, u32[]{:S(2)}) copy-start(f32[2,128,24,64]{1,3,2,0:T(8,128)S(1)} %get-tuple-element.3075) | copy-start | bytes 4718596
  1109.7 89.2 %copy-start.270 = (f32[2,24,128]{2,0,1:T(2,128)}, f32[2,24,128]{2,0,1:T(2,128)S(1)}, u32[]{:S(2)}) copy-start(f32[2,24,128]{2,0,1:T(2,128)S(1)} %get-tuple-element.3078) | copy-start | bytes 73732
  1109.7 89.2 %copy-start.314 = (f32[2,128,24,1]{1,2,0,3:T(8,128)}, f32[2,128,24,1]{1,2,0,3:T(8,128)S(1)}, u32[]{:S(2)}) copy-start(f32[2,128,24,1]{1,2,0,3:T(8,128)S(1)} %get-tuple-element.3061) | copy-start | bytes 73732
  1109.7 89.2 %copy-start.326 = (f32[256,24]{0,1:T(8,128)}, f32[256,24]{0,1:T(8,128)S(1)}, u32[]{:S(2)}) copy-start(f32[256,24]{0,1:T(8,128)S(1)} %get-tuple-element.3085) | copy-start | bytes 73732
  1109.7 89.2 %copy-start.543 = (f32[1,24]{1,0:T(1,128)}, f32[1,24]{1,0:T(1,128)S(1)}, u32[]{:S(2)}) copy-start(f32[1,24]{1,0:T(1,128)S(1)} %get-tuple-element.3083) | copy-start | bytes 292
  1109.7 92.7 %copy-start.519 = (f32[256,1]{0,1:T(1,128)}, f32[256,1]{0,1:T(1,128)S(1)}, u32[]{:S(2)}) copy-start(f32[256,1]{0,1:T(1,128)S(1)} %get-tuple-element.3060) | copy-start | bytes 3076
  1109.7 91.3 %copy-start.369 = (f32[1536]{0:T(1024)S(1)}, f32[1536]{0:T(1024)}, u32[]{:S(2)}) copy-start(f32[1536]{0:T(1024)} %copy-done.368) | copy-start | bytes 18436
  1237.7 80.2 %copy-start.208 = (f32[2,128,64]{1,0,2:T(2,128)S(1)}, f32[2,128,64]{1,0,2:T(2,128)}, u32[]{:S(2)}) copy-start(f32[2,128,64]{1,0,2:T(2,128)} %get-tuple-element.3067) | copy-start | bytes 196612
  1400.5 247.9 %reduce-scatter.33.cloned.1.call-start = ((), (), s32[]{:S(2)}) async-start(), calls=%async_computation.21 | async-start | bytes 835584
  1405.7 65.2 %copy-start.47 = (bf16[2,256,768]{2,1,0:T(8,128)(2,1)S(1)}, bf16[2,256,768]{2,1,0:T(8,128)(2,1)}, u32[]{:S(2)}) copy-start(bf16[2,256,768]{2,1,0:T(8,128)(2,1)} %param.87) | copy-start | bytes 2359300
  1405.7 65.1 %copy-start.216 = (f32[768]{0:T(1024)S(1)}, f32[768]{0:T(1024)}, u32[]{:S(2)}) copy-start(f32[768]{0:T(1024)} %copy-done.215) | copy-start | bytes 9220
  1405.8 65.1 %copy-start.334 = (f32[256]{0:T(256)S(1)}, f32[256]{0:T(256)}, u32[]{:S(2)}) copy-start(f32[256]{0:T(256)} %copy-done.333) | copy-start | bytes 3076
  1409.1 62.8 %copy-start.344 = (f32[256]{0:T(256)S(1)}, f32[256]{0:T(256)}, u32[]{:S(2)}) copy-start(f32[256]{0:T(256)} %copy-done.342) | copy-start | bytes 3076
  1409.1 63.8 %copy-start.141 = (f32[256,768]{1,0:T(8,128)S(1)}, f32[256,768]{1,0:T(8,128)}, u32[]{:S(2)}) copy-start(f32[256,768]{1,0:T(8,128)} %copy-done.140) | copy-start | bytes 2359300
  1409.1 63.8 %copy-start.478 = (f32[256]{0:T(256)S(1)}, f32[256]{0:T(256)}, u32[]{:S(2)}) copy-start(f32[256]{0:T(256)} %copy-done.476) | copy-start | bytes 3076
  1485.1 178.9 %reduce-scatter.27.cloned.1.call-start = ((), (), s32[]{:S(2)}) async-start(), calls=%async_computation.18 | async-start | bytes 417792
  1485.9 59.5 %copy-start.1 = (f32[256,1792]{1,0:T(8,128)S(1)}, f32[256,1792]{1,0:T(8,128)}, u32[]{:S(2)}) copy-start(f32[256,1792]{1,0:T(8,128)} %copy-done) | copy-start | bytes 5505028
  1485.9 59.5 %copy-start.447 = (f32[256]{0:T(256)S(1)}, f32[256]{0:T(256)}, u32[]{:S(2)}) copy-start(f32[256]{0:T(256)} %copy-done.444) | copy-start | bytes 3076
  1494.6 227.5 %reduce-scatter.25.cloned.1.call-start = ((), (), s32[]{:S(2)}) async-start(), calls=%async_computation.17 | async-start | bytes 417792
  1568.4 213.6 %reduce-scatter.31.cloned.1.call-start = ((), (), s32[]{:S(2)}) async-start(), calls=%async_computation.20 | async-start | bytes 974848
  1570.0 271.6 %reduce-scatter.29.cloned.1.call-start = ((), (), s32[]{:S(2)}) async-start(), calls=%async_computation.19 | async-start | bytes 974848
  1575.6 381.5 %reduce-scatter.23.cloned.1.call-start = ((), (), s32[]{:S(2)}) async-start(), calls=%async_computation.16 | async-start | bytes 10027008 | tf_op jit(solution)/shard_map/reduce_scatter | solution.py:192
  1586.6 486.1 %reduce-scatter.19.cloned.1.call-start = ((), (), s32[]{:S(2)}) async-start(), calls=%async_computation.14 | async-start | bytes 10027008 | tf_op jit(solution)/shard_map/reduce_scatter | solution.py:186
  1597.3 603.0 %reduce-scatter.21.cloned.1.call-start = ((), (), s32[]{:S(2)}) async-start(), calls=%async_computation.15 | async-start | bytes 11698176 | tf_op jit(solution)/shard_map/reduce_scatter | solution.py:187
  (447 other events, 2406.7 us)
Sparse Core Ops, SparseCore 0:
  10.9 46.7 all-gather.22
  60.6 45.5 all-gather.24
  109.0 39.9 all-gather.26
  151.1 42.7 all-gather.28
  196.0 40.7 all-gather.30
  239.0 41.0 all-gather.32
  1020.6 147.1 all-reduce.132
  1400.6 144.7 all-reduce.130
  1549.0 56.5 reduce-scatter.32
  1609.3 54.7 reduce-scatter.26
  1667.5 54.6 reduce-scatter.24
  1726.0 55.9 reduce-scatter.30
  1785.6 55.9 reduce-scatter.28
  1846.7 110.2 reduce-scatter.22
  1961.6 111.1 reduce-scatter.18
  2077.8 122.4 reduce-scatter.20
where the time goes:
time: 2230 us; the launch traced here: 2210 us
  waiting for transfers between devices  613 us (27%)
  local copies, waits for them, and re-layouts  379 us (17%)
  blocking collectives  326 us (15%)
  matrix products  308 us (14%)
  other arithmetic  295 us (13%)
  starting transfers between devices  190 us (9%)
  loops' own time  78 us (3%)
    ppermute x4, starting transfers between devices, partner(): return lax.ppermute(block, axis, route)  188 us
    unnamed x21, waiting for transfers between devices  186 us
    psum x2, blocking collectives, shards(): lax.psum((part_conv, part_step, part_bias, part_decay), 'dir')  147 us
    reduce_scatter x1, waiting for transfers between devices, scatter_grads(): lax.psum_scatter(totals[2], 'dp', scatter_dimension=1, tiled=True)  128 us
    reduce_scatter x1, waiting for transfers between devices, scatter_grads(): lax.psum_scatter(totals[1], 'dp', scatter_dimension=1, tiled=True)  116 us
    reduce_scatter x1, waiting for transfers between devices, scatter_grads(): lax.psum_scatter(totals[7], 'dp', scatter_dimension=1, tiled=True)  114 us
    dot_general x12, matrix products, block_scan(): jnp.einsum('chij,cjhp->cihp', mixing, heads_q, precision=lax.Precision.HI...  94.3 us
    another operation x12, loops' own time, own_way(): lax.cond(group == 0, lambda operands: direction(operands[0], operands[1],...  76.4 us
  transfers between devices with their start and end apart: 20, of which 9 were waited for; matrix products, arithmetic and copies ran while one was open for 28% of the time, Pallas kernels for 0%

commit v1 on v0

v1 whole, which is shorter than its diff:
```python
import functools
import jax
import jax.numpy as jnp
from jax import lax
from jax.experimental import pallas as pl
from jax.experimental.pallas import tpu as pltpu
from jax.sharding import PartitionSpec as P

BLK = 128
HD = 64
F32 = jnp.float32
BF16 = jnp.bfloat16
HIGH = lax.Precision.HIGHEST
LANES = 128


def mm(a, b):
    return lax.dot_general(a, b, (((1,), (0,)), ((), ())), preferred_element_type=F32)


def mm_nt(a, b):
    return lax.dot_general(a, b, (((1,), (1,)), ((), ())), preferred_element_type=F32)


def mm_tn(a, b):
    return lax.dot_general(a, b, (((0,), (0,)), ((), ())), preferred_element_type=F32)


def mm_exact(a, b):
    return lax.dot_general(
        a, b, (((1,), (0,)), ((), ())), precision=HIGH, preferred_element_type=F32
    )


def iota(shape, dim):
    return lax.broadcasted_iota(jnp.int32, shape, dim)


def square_masks():
    row, col = iota((BLK, BLK), 0), iota((BLK, BLK), 1)
    return row, col


def lag_keep(keep1, lag, rows=2 * BLK):
    at = iota((rows, 1), 0)
    first = (at >= lag).astype(F32)
    edge = ((at >= BLK) & (at < BLK + lag)).astype(F32)
    return first - edge * (1.0 - keep1)


def silu(v):
    return v * jax.nn.sigmoid(v)


class Sizes:
    def __init__(self, width, inner, convw, heads):
        self.D, self.E, self.CW, self.H = width, inner, convw, heads
        self.NP = inner + convw + LANES
        self.STEP = inner + convw
        self.T = 2 * BLK


def spread_matrix(sz, base):
    row = iota((LANES, sz.E), 0)
    col = iota((LANES, sz.E), 1)
    return (row % 64 == col // HD + base).astype(BF16)


def spread(values, matrix):
    high = values.astype(BF16).astype(F32)
    low = values - high
    lane = iota(values.shape, 1)
    packed = jnp.where(lane < 64, high, pltpu.roll(low, 64, 1)).astype(BF16)
    return mm(packed, matrix)


def conv_phase(sz, cin_of, taps, bias, keep1, out_ref, slope_ref):
    keeps = [None] + [lag_keep(keep1, k) for k in range(1, 4)]

    def chunk(n, _):
        at = pl.ds(pl.multiple_of(n * LANES, LANES), LANES)
        cin = cin_of(n)
        z = bias[:, at] + taps[0:1, at] * cin
        for k in range(1, 4):
            z = z + taps[k : k + 1, at] * (pltpu.roll(cin, k, 0) * keeps[k])
        sig = jax.nn.sigmoid(z)
        act = z * sig
        out_ref[:, at] = act
        if slope_ref is not None:
            slope_ref[:, at] = sig + act * (1.0 - sig)
        return 0

    lax.fori_loop(0, sz.CW // LANES, chunk, 0)


def step_phase(sz, raw, sbias, decay):
    z = raw + sbias
    dt = jnp.maximum(z, 0.0) + jnp.log1p(jnp.exp(-jnp.abs(z)))
    a = -dt * decay
    row, col = square_masks()
    lower = (row >= col).astype(F32)
    upper = (row <= col).astype(F32)
    lane = iota((BLK, LANES), 1)
    sums = []
    for b in range(2):
        part = a[b * BLK : (b + 1) * BLK]
        down, up = mm_exact(lower, part), mm_exact(upper, part)
        sums.append(jnp.where(lane < sz.H, down, up))
    return z, dt, a, sums


def b_and_c(sz, conv_ref):
    lane = iota((sz.T, LANES), 1)
    out = []
    for way in range(2):
        pair = conv_ref[:, sz.E + way * LANES : sz.E + (way + 1) * LANES]
        bp = jnp.where(lane < 64, pair, 0.0)
        cp = jnp.where(lane < 64, pltpu.roll(pair, 64, 1), 0.0)
        cp = pltpu.roll(cp, 1 if way == 0 else sz.T - 1, 0)
        out.append((bp.astype(BF16), cp.astype(BF16)))
    return out


def blk(v, b):
    return v[b * BLK : (b + 1) * BLK]


def carry_weights(sz, dt, sums):
    end0 = jnp.exp(sums[0][BLK - 1 : BLK, :] - sums[0])
    end1 = jnp.exp(sums[1][0:1, :] - sums[1])
    lane = iota((BLK, LANES), 1)
    fwd = jnp.where(lane < sz.H, end0, 0.0)
    rev = jnp.where((lane >= sz.H) & (lane < 2 * sz.H), end1, 0.0)
    return fwd, rev


def forward_scan(sz, conv_ref, y_ref, colb, rowt, bc, dt, a, sums, keep1, spreads):
    row, col = square_masks()
    low = row > col
    (bf, cf), (bb, cb) = bc
    excl = [sums[b] - blk(a, b) for b in range(2)]
    scores = []
    for b in range(2):
        sf = mm_nt(blk(cf, b), blk(bf, b))
        sb = mm_nt(blk(cb, b), blk(bb, b))
        scores.append(jnp.where(low, sf, jnp.where(row < col, sb, 0.0)))
        rowt[0, b] = sums[b].T
        rowt[1, b] = blk(dt, b).T
        for h in range(sz.H):
            ef = jnp.broadcast_to(excl[b][:, h : h + 1], (BLK, BLK))
            eb = jnp.broadcast_to(excl[b][:, sz.H + h : sz.H + h + 1], (BLK, BLK))
            colb[0, h, b * BLK : (b + 1) * BLK] = jnp.where(low, ef, eb)
    left = iota((BLK, LANES), 1) < HD

    def pair(p, _):
        at = pl.ds(pl.multiple_of(p * LANES, LANES), LANES)
        for b in range(2):
            rows = slice(b * BLK, (b + 1) * BLK)
            x = conv_ref[rows, at].astype(BF16)
            ys = []
            for hh in range(2):
                h = 2 * p + hh
                sum_row = jnp.where(low, rowt[0, b, pl.ds(h, 1)], rowt[0, b, pl.ds(sz.H + h, 1)])
                dt_row = jnp.where(low, rowt[1, b, pl.ds(h, 1)], rowt[1, b, pl.ds(sz.H + h, 1)])
                decay = jnp.exp(jnp.minimum(colb[0, h, rows] - sum_row, 0.0))
                mix = decay * scores[b] * dt_row
                ys.append(mm(mix.astype(BF16), x))
            y_ref[rows, at] = jnp.where(left, ys[0], ys[1])
        return 0

    lax.fori_loop(0, sz.H // 2, pair, 0)
    states = carry_states(sz, conv_ref, bc, dt, sums, keep1, spreads)
    y_ref[BLK:, :] += mm(blk(cf, 1), states[0]) * spread(jnp.exp(excl[1]), spreads[0])
    y_ref[:BLK, :] += mm(blk(cb, 0), states[1]) * spread(jnp.exp(excl[0]), spreads[1])


def carry_states(sz, conv_ref, bc, dt, sums, keep1, spreads):
    (bf, _), (bb, _) = bc
    fwd, rev = carry_weights(sz, dt, sums)
    xf = conv_ref[:BLK, : sz.E] * spread(fwd * blk(dt, 0), spreads[0])
    xb = conv_ref[BLK:, : sz.E] * spread(rev * blk(dt, 1), spreads[1])
    sf = mm_tn(blk(bf, 0), xf.astype(BF16)) * keep1
    sb = mm_tn(blk(bb, 1), xb.astype(BF16)) * keep1
    return sf.astype(BF16), sb.astype(BF16)


ROWS = 16


def row_loop(sz, body, init):
    def step(n, carry):
        return body(pl.ds(pl.multiple_of(n * ROWS, ROWS), ROWS), n, carry)

    return lax.fori_loop(0, sz.T // ROWS, step, init)


def live_rows(n, live1):
    later = (n >= BLK // ROWS).astype(F32)
    return 1.0 + later * (live1 - 1.0)


def norm_in(sz, u_ref, gain, normed_ref):
    def body(at, n, _):
        u = u_ref[at, :].astype(F32)
        r = lax.rsqrt(jnp.mean(u * u, axis=-1, keepdims=True) + 1e-05)
        normed_ref[at, :] = (u * r * gain[...]).astype(BF16)
        return 0

    row_loop(sz, body, 0)


def project(sz, normed_ref, win_ref, proj_ref, cols=None):
    width = sz.NP // 9
    normed = normed_ref[...]
    for n in range(9):
        proj_ref[:, n * width : (n + 1) * width] = mm(normed, win_ref[:, n * width : (n + 1) * width])


def gate_mix(sz, at, y_ref, conv_ref, proj_ref, skipw):
    x = conv_ref[at, : sz.E]
    gate = proj_ref[at, : sz.E]
    mixed = y_ref[at, :] + x * skipw[...]
    sig = jax.nn.sigmoid(gate)
    act = gate * sig
    gated = mixed * act
    scale = lax.rsqrt(jnp.mean(gated * gated, axis=-1, keepdims=True) + 1e-05)
    return x, gate, mixed, sig, act, gated, scale


def post_mix(sz, y_ref, conv_ref, proj_ref, skipw, gain, nout_ref):
    def body(at, n, _):
        _, _, _, _, _, gated, scale = gate_mix(sz, at, y_ref, conv_ref, proj_ref, skipw)
        nout_ref[at, :] = (gated * scale * gain[...]).astype(BF16)
        return 0

    row_loop(sz, body, 0)


def forward_layer(sz, p, flags, u_ref, win_ref, wout_ref, proj_ref, y_ref, unext_ref, conv_ref,
                  normed_ref, nout_ref, colb, rowt, slope_ref=None, hook=lambda n: None):
    keep1, live1 = flags[0], flags[1]
    norm_in(sz, u_ref, p["gain_in"], normed_ref)
    hook(0)
    project(sz, normed_ref, win_ref, proj_ref)
    hook(1)
    cin_of = lambda n: proj_ref[:, pl.ds(pl.multiple_of(sz.E + n * LANES, LANES), LANES)]
    conv_phase(sz, cin_of, p["taps"], p["cbias"], keep1, conv_ref, slope_ref)
    hook(2)
    _, dt, a, sums = step_phase(sz, proj_ref[:, sz.STEP :], p["sbias"][...], p["decay"][...])
    spreads = (spread_matrix(sz, 0), spread_matrix(sz, sz.H))
    bc = b_and_c(sz, conv_ref)
    forward_scan(sz, conv_ref, y_ref, colb, rowt, bc, dt, a, sums, keep1, spreads)
    hook(3)
    post_mix(sz, y_ref, conv_ref, proj_ref, p["skipw"], p["gain_out"], nout_ref)
    hook(4)
    branch = mm(nout_ref[...], wout_ref[...])
    unext_ref[:BLK, :] = u_ref[:BLK, :].astype(F32) + branch[:BLK]
    unext_ref[BLK:, :] = u_ref[BLK:, :].astype(F32) + live1 * branch[BLK:]


def fold8(v):
    out = v[0:8]
    for n in range(1, v.shape[0] // 8):
        out = out + v[n * 8 : (n + 1) * 8]
    return out


def colsum(v):
    return jnp.sum(v, axis=0, keepdims=True)


def backward_scan(sz, conv_ref, gy_ref, gx_ref, gbc_ref, colb, rowt, accs, z, dt, a, sums, keep1,
                  spreads, decay, hook):
    row, col = square_masks()
    low = row < col
    bc = b_and_c(sz, conv_ref)
    (bf, cf), (bb, cb) = bc
    excl = [sums[b] - blk(a, b) for b in range(2)]
    scores = []
    for b in range(2):
        sf = mm_nt(blk(bf, b), blk(cf, b))
        sb = mm_nt(blk(bb, b), blk(cb, b))
        scores.append(jnp.where(low, sf, jnp.where(row > col, sb, 0.0)))
        rowt[0, b] = excl[b].T
        here = slice(b * BLK, (b + 1) * BLK)
        for h in range(sz.H):
            for n, v in ((0, sums[b]), (1, blk(dt, b))):
                vf = jnp.broadcast_to(v[:, h : h + 1], (BLK, BLK))
                vb = jnp.broadcast_to(v[:, sz.H + h : sz.H + h + 1], (BLK, BLK))
                colb[n, h, here] = jnp.where(low, vf, vb)
    gscore, rho_ref, kappa_ref = accs
    gscore[...] = jnp.zeros_like(gscore)
    kappa_ref[...] = jnp.zeros_like(kappa_ref)
    rho_ref[...] = jnp.zeros_like(rho_ref)
    lane = iota((BLK, LANES), 1)
    left = lane < HD

    def pair(p, _):
        at = pl.ds(pl.multiple_of(p * LANES, LANES), LANES)
        for b in range(2):
            rows = slice(b * BLK, (b + 1) * BLK)
            x = conv_ref[rows, at]
            gy = gy_ref[rows, at]
            x_two = jnp.concatenate([jnp.where(left, x, 0.0), jnp.where(left, 0.0, x)], axis=0)
            w_two = mm_nt(x_two.astype(BF16), gy)
            gxs = []
            gs = gscore[rows]
            kap = kappa_ref[rows]
            for hh in range(2):
                h = 2 * p + hh
                ex_row = jnp.where(low, rowt[0, b, pl.ds(h, 1)], rowt[0, b, pl.ds(sz.H + h, 1)])
                decay_m = jnp.exp(jnp.minimum(ex_row - colb[0, h, rows], 0.0))
                dtc = colb[1, h, rows]
                w = w_two[hh * BLK : (hh + 1) * BLK]
                es = decay_m * scores[b]
                gxs.append(mm((es * dtc).astype(BF16), gy))
                gs = gs + decay_m * w * dtc
                r = es * w
                q = r * dtc
                rl = jnp.where(low, r, 0.0)
                kap = jnp.where(lane == h, jnp.sum(rl, axis=1, keepdims=True), kap)
                kap = jnp.where(lane == sz.H + h, jnp.sum(r - rl, axis=1, keepdims=True), kap)
                ql = jnp.where(low, q, 0.0)
                rho_ref[b, pl.ds(h, 1)] = colsum(ql)
                rho_ref[b, pl.ds(sz.H + h, 1)] = colsum(q - ql)
            gscore[rows] = gs
            kappa_ref[rows] = kap
            gx_ref[rows, at] += jnp.where(left, gxs[0], gxs[1])
        hook(p)
        return 0

    lax.fori_loop(0, sz.H // 2, pair, 0)

    states = carry_states(sz, conv_ref, bc, dt, sums, keep1, spreads)
    ends = carry_weights(sz, dt, sums)
    values, enters = [], []
    gbs, gcs = [], []
    for way in range(2):
        src, dst = (0, 1) if way == 0 else (1, 0)
        bw, cw = bc[way]
        rows_s = slice(src * BLK, (src + 1) * BLK)
        rows_d = slice(dst * BLK, (dst + 1) * BLK)
        gcar = gy_ref[rows_d, :].astype(F32) * spread(jnp.exp(excl[dst]), spreads[way])
        gcar_low = gcar.astype(BF16)
        inner = mm(blk(cw, dst), states[way])
        enters.append(mm_nt((gcar * inner).astype(BF16), spreads[way]))
        gstate = (mm_tn(blk(cw, dst), gcar_low) * keep1).astype(BF16)
        gc_d = mm_nt(gcar_low, states[way])
        weight = spread(ends[way] * blk(dt, src), spreads[way])
        x = conv_ref[rows_s, : sz.E]
        gb_s = mm_nt((x * weight).astype(BF16), gstate)
        bg = mm(blk(bw, src), gstate)
        gx_ref[rows_s, :] += weight * bg
        values.append(mm_nt((x * bg).astype(BF16), spreads[way]))
        gb, gc = [None, None], [None, None]
        for b in range(2):
            g = gscore[b * BLK : (b + 1) * BLK]
            g = jnp.where(low if way == 0 else row > col, g, 0.0).astype(BF16)
            gb[b] = mm(g, blk(cw, b))
            gc[b] = mm_tn(g, blk(bw, b))
        gb[src] = gb[src] + gb_s
        gc[dst] = gc[dst] + gc_d
        gc_all = jnp.concatenate(gc, axis=0)
        at = iota((sz.T, 1), 0)
        if way == 0:
            gc_all = jnp.where(at == sz.T - 1, 0.0, pltpu.roll(gc_all, sz.T - 1, 0))
        else:
            gc_all = jnp.where(at == 0, 0.0, pltpu.roll(gc_all, 1, 0))
        gb_all = jnp.concatenate(gb, axis=0)
        wide_lane = iota((sz.T, LANES), 1)
        gbc_ref[:, way * LANES : (way + 1) * LANES] = jnp.where(
            wide_lane < 64, gb_all, pltpu.roll(gc_all, 64, 1)
        )

    strict_low = (row > col).astype(F32)
    strict_up = (row < col).astype(F32)
    is_f = lane < sz.H
    is_b = (lane >= sz.H) & (lane < 2 * sz.H)
    gsteps, gdecay = [], None
    for b in range(2):
        kr = kappa_ref[b * BLK : (b + 1) * BLK]
        kap = kr * blk(dt, b)
        rho = rho_ref[b].T
        if b == 1:
            rho = rho + jnp.where(is_f, enters[0], 0.0)
            zr = jnp.where(is_b, values[1], 0.0) * ends[1]
        else:
            rho = rho + jnp.where(is_b, enters[1], 0.0)
            zr = jnp.where(is_f, values[0], 0.0) * ends[0]
        zed = zr * blk(dt, b)
        diff = rho - kap
        both = jnp.concatenate([diff, zed], axis=1)
        up, down = mm_exact(strict_up, both), mm_exact(strict_low, both)
        ga = jnp.where(
            is_f, up[:, :LANES] + down[:, LANES:], down[:, :LANES] + up[:, LANES:]
        ) - kap
        ga = jnp.where(is_f | is_b, ga, 0.0)
        gdt = jnp.where(is_f | is_b, kr + zr, 0.0) - ga * decay
        gsteps.append(gdt * jax.nn.sigmoid(blk(z, b)))
        part = colsum(ga * blk(a, b))
        gdecay = part if gdecay is None else gdecay + part
    return jnp.concatenate(gsteps, axis=0), gdecay


def backward_layer(sz, p, flags, g_ref, u_ref, win_ref, wout_ref, proj_ref, y_ref, gu_ref,
                   gwin_ref, gwout_ref, small_ref, head_ref, s, hook=lambda n: None,
                   recompute=True):
    keep1, live1 = flags[0], flags[1]
    conv_ref, slope_ref = s["conv"], s["slope"]
    D, E, CW = sz.D, sz.E, sz.CW
    if recompute:
        cin_of = lambda n: proj_ref[:, pl.ds(pl.multiple_of(E + n * LANES, LANES), LANES)]
        conv_phase(sz, cin_of, p["taps"], p["cbias"], keep1, conv_ref, slope_ref)
        norm_in(sz, u_ref, p["gain_in"], s["normed"])
    hook(0)

    def mask_g(at, n, _):
        s["gb"][at, :] = (g_ref[at, :].astype(F32) * live_rows(n, live1)).astype(BF16)
        return 0

    row_loop(sz, mask_g, 0)
    s["gx"][...] = mm_nt(s["gb"][...], wout_ref[...])
    hook(1)
    s["acc"][...] = jnp.zeros_like(s["acc"])

    def post_back(at, n, _):
        x, gate, mixed, sig, act, gated, scale = gate_mix(sz, at, y_ref, conv_ref, proj_ref, p["skipw"])
        hat = gated * scale
        gn = s["gx"][at, :]
        s["acc"][0] += fold8(gn * hat)
        s["nout"][at, :] = (hat * p["gain_out"][...]).astype(BF16)
        gh = gn * p["gain_out"][...]
        gg = scale * (gh - hat * jnp.mean(gh * hat, axis=-1, keepdims=True))
        gm = gg * act
        s["gproj"][at, :E] = (gg * mixed * (sig + act * (1.0 - sig))).astype(BF16)
        s["gy"][at, :] = gm.astype(BF16)
        s["gx"][at, :] = gm * p["skipw"][...]
        s["acc"][1] += fold8(gm * x)
        return 0

    row_loop(sz, post_back, 0)
    hook(2)
    small_ref[6:7, :E] = colsum(s["acc"][0])
    gwout_ref[...] = mm_tn(s["nout"][...], s["gb"][...]).astype(BF16)
    hook(3)
    spreads = (spread_matrix(sz, 0), spread_matrix(sz, sz.H))
    z, dt, a, sums = step_phase(sz, proj_ref[:, sz.STEP :], p["sbias"][...], p["decay"][...])
    gsteps, gdecay = backward_scan(
        sz, conv_ref, s["gy"], s["gx"], s["gbc"], s["colb"], s["rowt"],
        (s["gscore"], s["rho"], s["kappa"]), z, dt, a, sums, keep1, spreads, p["decay"][...],
        lambda n: None,
    )
    hook(4)
    s["gproj"][:, sz.STEP :] = gsteps.astype(BF16)
    skip_sum = s["acc"][1]
    first = skip_sum.astype(BF16)
    rest = (skip_sum - first.astype(F32)).astype(BF16)
    gskip = colsum(mm_nt(first, spreads[0]) + mm_nt(rest, spreads[0]))
    head_ref[...] = jnp.zeros_like(head_ref)
    head_ref[0:1, :] = colsum(gsteps)
    head_ref[1:2, :] = gdecay
    head_ref[2:3, :] = gskip

    keeps = [None] + [lag_keep(keep1, k) for k in range(1, 4)]

    def conv_chunk(n, gout):
        at = pl.ds(pl.multiple_of(n * LANES, LANES), LANES)
        wide = pl.ds(pl.multiple_of(E + n * LANES, LANES), LANES)
        cin = proj_ref[:, wide]
        gz = gout * slope_ref[:, at]
        taps = p["taps"]
        gc = taps[0:1, at] * gz
        small_ref[1:2, at] = colsum(gz * cin)
        for k in range(1, 4):
            gk = gz * keeps[k]
            small_ref[1 + k : 2 + k, at] = colsum(gk * pltpu.roll(cin, k, 0))
            gc = gc + taps[k : k + 1, at] * pltpu.roll(gk, sz.T - k, 0)
        small_ref[5:6, at] = colsum(gz)
        s["gproj"][:, wide] = gc.astype(BF16)

    def x_chunk(n, _):
        conv_chunk(n, s["gx"][:, pl.ds(pl.multiple_of(n * LANES, LANES), LANES)])
        return 0

    lax.fori_loop(0, E // LANES, x_chunk, 0)
    for n in range((CW - E) // LANES):
        conv_chunk(E // LANES + n, s["gbc"][:, n * LANES : (n + 1) * LANES])
    hook(5)
    width = sz.NP // 9
    normed = s["normed"][...]
    total = None
    for n in range(9):
        cols = slice(n * width, (n + 1) * width)
        gp = s["gproj"][:, cols]
        gwin_ref[:, cols] = mm_tn(normed, gp).astype(BF16)
        part = mm_nt(gp, win_ref[:, cols])
        total = part if total is None else total + part
    s["gn"][...] = total
    hook(6)
    s["acc"][0] = jnp.zeros_like(s["acc"][0])

    def in_back(at, n, _):
        u = u_ref[at, :].astype(F32)
        r = lax.rsqrt(jnp.mean(u * u, axis=-1, keepdims=True) + 1e-05)
        hat = u * r
        gn = s["gn"][at, :]
        s["acc"][0, :, :D] += fold8(gn * hat)
        gh = gn * p["gain_in"][...]
        gu = r * (gh - hat * jnp.mean(gh * hat, axis=-1, keepdims=True))
        gu_ref[at, :] = g_ref[at, :].astype(F32) + gu
        return 0

    row_loop(sz, in_back, 0)
    small_ref[0:1, :D] = colsum(s["acc"][0, :, :D])
    hook(7)


def backward_scratch(sz):
    T, E, CW, D, H = sz.T, sz.E, sz.CW, sz.D, sz.H
    return dict(
        conv=pltpu.VMEM((T, CW), F32),
        slope=pltpu.VMEM((T, CW), F32),
        normed=pltpu.VMEM((T, D), BF16),
        gb=pltpu.VMEM((T, D), BF16),
        gx=pltpu.VMEM((T, E), F32),
        gy=pltpu.VMEM((T, E), BF16),
        nout=pltpu.VMEM((T, E), BF16),
        gproj=pltpu.VMEM((T, sz.NP), BF16),
        gbc=pltpu.VMEM((T, 2 * LANES), F32),
        gn=pltpu.VMEM((T, D), F32),
        acc=pltpu.VMEM((2, 8, E), F32),
        colb=pltpu.VMEM((2, H, T, BLK), F32),
        rowt=pltpu.VMEM((2, 2, LANES, BLK), F32),
        gscore=pltpu.VMEM((T, BLK), F32),
        rho=pltpu.VMEM((2, LANES, BLK), F32),
        kappa=pltpu.VMEM((T, LANES), F32),
    )


PARAMS = ("gain_in", "taps", "cbias", "sbias", "decay", "skipw", "gain_out")


VM = pl.BlockSpec(memory_space=pltpu.VMEM)
SM = pl.BlockSpec(memory_space=pltpu.SMEM)
ROOM = 62 << 20


def fwd_kernel(sz, flags, u, win, wout, *rest):
    p = dict(zip(PARAMS, rest[:7]))
    proj, y, unext = rest[7:10]
    conv, normed, nout, colb, rowt = rest[10:]
    forward_layer(sz, p, flags, u, win, wout, proj, y, unext, conv, normed, nout, colb, rowt)


def forward_scratch(sz):
    return [
        pltpu.VMEM((sz.T, sz.CW), F32),
        pltpu.VMEM((sz.T, sz.D), BF16),
        pltpu.VMEM((sz.T, sz.E), BF16),
        pltpu.VMEM((1, sz.H, sz.T, BLK), F32),
        pltpu.VMEM((2, 2, LANES, BLK), F32),
    ]


def fwd_call(sz, flags, u, win, wout, params):
    return pl.pallas_call(
        functools.partial(fwd_kernel, sz),
        out_shape=[
            jax.ShapeDtypeStruct((sz.T, sz.NP), F32),
            jax.ShapeDtypeStruct((sz.T, sz.E), F32),
            jax.ShapeDtypeStruct((sz.T, sz.D), F32),
        ],
        in_specs=[SM] + [VM] * 10,
        out_specs=[VM] * 3,
        scratch_shapes=forward_scratch(sz),
        compiler_params=pltpu.CompilerParams(vmem_limit_bytes=ROOM),
    )(flags, u, win, wout, *params)


def bwd_kernel(sz, names, flags, g, u, win, wout, proj, y, *rest):
    p = dict(zip(PARAMS, rest[:7]))
    gu, gwin, gwout, small, head = rest[7:12]
    s = dict(zip(names, rest[12:]))
    backward_layer(sz, p, flags, g, u, win, wout, proj, y, gu, gwin, gwout, small, head, s)


def grad_shapes(sz):
    return [
        jax.ShapeDtypeStruct((sz.T, sz.D), F32),
        jax.ShapeDtypeStruct((sz.D, sz.NP), BF16),
        jax.ShapeDtypeStruct((sz.E, sz.D), BF16),
        jax.ShapeDtypeStruct((8, sz.CW), F32),
        jax.ShapeDtypeStruct((8, LANES), F32),
    ]


def bwd_call(sz, flags, g, u, win, wout, proj, y, params):
    s = backward_scratch(sz)
    return pl.pallas_call(
        functools.partial(bwd_kernel, sz, tuple(s)),
        out_shape=grad_shapes(sz),
        in_specs=[SM] + [VM] * 13,
        out_specs=[VM] * 5,
        scratch_shapes=list(s.values()),
        compiler_params=pltpu.CompilerParams(vmem_limit_bytes=ROOM),
    )(flags, g, u, win, wout, proj, y, *params)


def run_flags(lengths):
    ends = jnp.cumsum(lengths)
    begins = ends - lengths
    opens = jnp.any((begins == 1) & (lengths > 0)) | (ends[-1] <= 1)
    return jnp.stack([1.0 - opens.astype(F32), (ends[-1] > 1).astype(F32)])


def pad_lanes(v, width=LANES):
    return jnp.pad(v, [(0, 0)] * (v.ndim - 1) + [(0, width - v.shape[-1])])


def small_pack(in_gain, conv_weight, conv_bias, out_gain):
    layers, taps = conv_weight.shape[:2]
    rows = [
        pad_lanes(in_gain),
        pad_lanes(conv_weight.reshape(layers * taps, -1)),
        pad_lanes(conv_bias),
        pad_lanes(out_gain),
    ]
    packed = jnp.concatenate(rows, axis=0)
    return jnp.pad(packed, ((0, -packed.shape[0] % 16), (0, 0)))


def small_unpack(gathered, layers, taps, sizes):
    gathered = gathered.astype(F32)

    def rows(first, count, n):
        part = gathered[:, first : first + count, :n]
        return part.transpose(1, 0, 2).reshape(count, -1)

    n_in, n_conv, n_out = sizes
    gain_in = rows(0, layers, n_in)
    taps_all = rows(layers, layers * taps, n_conv).reshape(layers, taps, -1)
    bias = rows(layers * (1 + taps), layers, n_conv)
    gain_out = rows(layers * (2 + taps), layers, n_out)
    return gain_in, taps_all, bias, gain_out


def shards(resid_in, grad_out, seq_spans, in_gain, w_gate_in, w_conv_in, w_step, conv_weight,
           conv_bias, step_bias, decay_log, skip_gain, out_gain, w_out):
    layers, taps = conv_weight.shape[:2]
    ndp = lax.axis_size("dp")
    me_dir, me = lax.axis_index("dir"), lax.axis_index("dp")
    width, inner, convw = resid_in.shape[2], w_gate_in.shape[2], w_conv_in.shape[2]
    heads = skip_gain.shape[1]
    sz = Sizes(width, inner, convw, heads)
    pick = lambda v: lax.dynamic_index_in_dim(v, me_dir, 0, keepdims=False)
    u0, g1 = pick(resid_in), pick(grad_out)
    flags = run_flags(pick(seq_spans))

    win_shard = jnp.concatenate([w_gate_in, w_conv_in, pad_lanes(w_step)], axis=2)
    packed = small_pack(in_gain, conv_weight, conv_bias, out_gain)
    sizes = (in_gain.shape[1], conv_weight.shape[2], out_gain.shape[1])
    gain_in, taps_all, bias, gain_out = small_unpack(
        lax.all_gather(packed, "dp"), layers, taps, sizes
    )
    win = [lax.all_gather(win_shard[l], "dp", axis=0, tiled=True) for l in range(layers)]
    wout = [lax.all_gather(w_out[l], "dp", axis=0, tiled=True) for l in range(layers)]
    decay = jnp.exp(decay_log)
    decay = pad_lanes(jnp.concatenate([decay, decay], axis=1))
    sbias = pad_lanes(step_bias)
    skipw = jnp.repeat(skip_gain, inner // heads, axis=1)
    params = [
        [gain_in[l][None], taps_all[l], bias[l][None], sbias[l][None], decay[l][None],
         skipw[l][None], gain_out[l][None]]
        for l in range(layers)
    ]

    u, saved = u0, []
    for l in range(layers):
        proj, y, unext = fwd_call(sz, flags, u, win[l], wout[l], params[l])
        saved.append((u, proj, y))
        u = unext
    resid = lax.all_gather(u.astype(BF16), "dir")

    g = g1
    grads = [None] * layers
    for l in reversed(range(layers)):
        u, proj, y = saved[l]
        g, gwin, gwout, small, head = bwd_call(
            sz, flags, g, u, win[l], wout[l], proj, y, params[l]
        )
        gwin = lax.psum_scatter(gwin, "dp", scatter_dimension=0, tiled=True)
        gwout = lax.psum_scatter(gwout, "dp", scatter_dimension=0, tiled=True)
        grads[l] = (gwin, gwout, small, head)
    grad_in = lax.all_gather(g, "dir")
    gwin = lax.psum(jnp.stack([v[0] for v in grads]).astype(F32), "dir")
    gwout = lax.psum(jnp.stack([v[1] for v in grads]).astype(F32), "dir")
    small, head = lax.psum(
        (jnp.stack([v[2] for v in grads]), jnp.stack([v[3] for v in grads])), ("dir", "dp")
    )

    def own(v, n):
        return lax.dynamic_slice_in_dim(v, me * n, n, axis=v.ndim - 1)

    return (
        resid,
        grad_in,
        own(small[:, 0, :width], sizes[0]),
        gwin[:, :, :inner],
        gwin[:, :, inner : inner + convw],
        gwin[:, :, inner + convw : inner + convw + 2 * heads],
        own(small[:, 1 : 1 + taps], sizes[1]),
        own(small[:, 5], sizes[1]),
        head[:, 0, : 2 * heads],
        head[:, 1, :heads] + head[:, 1, heads : 2 * heads],
        head[:, 2, :heads],
        own(small[:, 6, :inner], sizes[2]),
        gwout,
    )


def solution(mesh):
    rows, cols, last = P(None, "dp", None), P(None, "dp"), P(None, None, "dp")
    placed = (rows, rows, cols, cols, rows, rows, rows, last, cols, P(), P(), P(), cols, rows)
    out = (rows, rows, cols, rows, rows, rows, last, cols, P(), P(), P(), cols, rows)
    return jax.shard_map(shards, mesh=mesh, in_specs=placed, out_specs=out, check_vma=False)
```

time: 2230 us -> 810 us (0.36)
  local copies, waits for them, and re-layouts: 379 us -> 27.9 us
  matrix products: 308 us -> 0 us
  other arithmetic: 295 us -> 8.1 us
  blocking collectives: 326 us -> 72.9 us
  starting transfers between devices: 190 us -> 0.44 us
  Pallas kernels: 0 us -> 114 us
  loops' own time: 78 us -> 0 us
  waiting for transfers between devices: 613 us -> 559 us
    dot_general x108 -> x0, matrix products: 308 us -> none  [the longest x12 94.3 us: block_scan(): jnp.einsum('chij,cjhp->cihp', mixing, heads_q, precision=lax.Precision.HI...]
    ppermute x4 -> x0, starting transfers between devices: 188 us -> none  [partner(): return lax.ppermute(block, axis, route)]
    unnamed x21 -> x11, waiting for transfers between devices: 186 us -> 3.2 us
    all_gather x6 -> x5, waiting for transfers between devices: 0.05 us -> 171 us  [the longest x2 116 us: shards(): lax.all_gather(win_shard[l], 'dp', axis=0, tiled=True)]
    psum x3 -> x1, blocking collectives: 181 us -> 39.6 us  [shards(): lax.psum((jnp.stack([v[2] for v in grads]), jnp.stack([v[3] for v in grad...]
    pallas_call x0 -> x4, Pallas kernels: none -> 114 us  [the longest x2 76.7 us: bwd_call(): pl.pallas_call(functools.partial(bwd_kernel, sz, tuple(s)), out_shape=gra...]
    reduce_scatter x3 -> x4, waiting for transfers between devices: 357 us -> 250 us  [the longest x2 164 us: shards(): gwin = lax.psum_scatter(gwin, 'dp', scatter_dimension=0, tiled=True)]
    slice x37 -> x25, local copies, waits for them, and re-layouts: 112 us -> 17.5 us  [the longest x1 2.11 us: shards(): gwin[:, :, inner:inner + convw]]
  transfers between devices with their start and end apart: 20 -> 11, of which waited for: 9 -> 11; matrix products, arithmetic and copies ran while one was open for 28% -> 3% of each run, Pallas kernels for 0% -> 7%
where the time goes in v1:
time: 810 us; the launch traced here: 800 us
  waiting for transfers between devices  559 us (69%)
  Pallas kernels  114 us (14%)
  blocking collectives  72.9 us (9%)
  local copies, waits for them, and re-layouts  27.9 us (3%)
  between operations  16.6 us (2%)
  other arithmetic  8.1 us (1%)
    reduce_scatter x2, waiting for transfers between devices, shards(): gwin = lax.psum_scatter(gwin, 'dp', scatter_dimension=0, tiled=True)  164 us
    all_gather x2, waiting for transfers between devices, shards(): lax.all_gather(win_shard[l], 'dp', axis=0, tiled=True)  116 us
    reduce_scatter x2, waiting for transfers between devices, shards(): gwout = lax.psum_scatter(gwout, 'dp', scatter_dimension=0, tiled=True)  86.5 us
    pallas_call x2, Pallas kernels, bwd_call(): pl.pallas_call(functools.partial(bwd_kernel, sz, tuple(s)), out_shape=gra...  76.7 us
    psum x1, waiting for transfers between devices, shards(): lax.psum((jnp.stack([v[2] for v in grads]), jnp.stack([v[3] for v in grad...  72.5 us
    psum x1, waiting for transfers between devices, shards(): gwin = lax.psum(jnp.stack([v[0] for v in grads]).astype(F32), 'dir')  62.7 us
    psum x1, blocking collectives, shards(): lax.psum((jnp.stack([v[2] for v in grads]), jnp.stack([v[3] for v in grad...  39.6 us
    pallas_call x2, Pallas kernels, fwd_call(): pl.pallas_call(functools.partial(fwd_kernel, sz), out_shape=[jax.ShapeDty...  37.6 us
  transfers between devices with their start and end apart: 11, of which 11 were waited for; matrix products, arithmetic and copies ran while one was open for 3% of the time, Pallas kernels for 7%

profile of v1, /device:TPU:0, one launch (start us, length us, event | category | flops | bytes accessed | tf_op | source)
XLA Modules:
  0.0 799.6 jit_solution(3604035032640159697)
XLA Ops:
  7.2 1.8 fusion.13
  9.1 1.1 fusion.1
  10.3 0.9 fusion.12
  11.3 0.7 all-gather.19.cloned.1.call-update
  12.0 0.5 all-gather.17.cloned.1.call-update
  12.6 0.2 reduce-window.4
  12.8 0.6 slice.132
  14.7 0.6 and_reduce_fusion
  16.1 23.4 %all-gather.2 = bf16[256,128]{1,0:T(8,128)(2,1)S(1)} all-gather(bf16[16,128]{1,0:T(8,128)(2,1)S(1)} %pad.36), channel_id=4, replica_groups=mesh['dir'=2,'dp'=16] {'dp'}, dimensions={0}, use_global_device_ids=true | all-gather | bytes 69632 | tf_op jit(solution)/shard_map/all_gather | solution.py:663
  39.5 0.7 slice.137.rest_0_
  40.3 0.7 squeeze.46.rest_1_
  41.0 0.7 slice.142.rest_2_
  41.8 0.7 broadcast_in_dim.10.rest_5_
  42.5 0.7 slice.149.rest_6_
  43.2 0.7 slice.153.rest_0_
  43.9 0.7 squeeze.49.rest_1_
  44.6 0.7 slice.156.rest_2_
  45.3 0.7 broadcast_in_dim.12.rest_5_
  46.0 0.7 slice.162.rest_6_
  46.7 0.6 pad_maximum_fusion.2.flags
  47.3 0.1 select_maximum_fusion
  47.3 0.8 dynamic-slice_bitcast_fusion.1.u
  48.1 0.8 dynamic-slice_bitcast_fusion.g
  48.9 0.5 pad_slice_fusion
  49.4 6.7 all-gather.15.cloned.1.call-done
  56.1 57.9 %all-gather.13.cloned.1.call-done = bf16[1,768,3456]{2,1,0:T(8,128)(2,1)} async-done(((bf16[1,48,3456]{2,1,0:T(8,128)(2,1)}), bf16[1,768,3456]{2,1,0:T(8,128)(2,1)}) %all-gather.13.cloned.1.call-update) | async-done | bytes 5308432 | tf_op jit(solution)/shard_map/all_gather | solution.py:665
  114.1 18.8 %shard_map.237 = (f32[256,3456]{1,0:T(8,128)}, f32[256,1536]{1,0:T(8,128)}, f32[256,768]{1,0:T(8,128)}) custom-call(f32[2]{0:T(128)} %pad_maximum_fusion.2.flags, bf16[256,768]{1,0:T(8,128)(2,1)} %dynamic-slice_bitcast_fusion.1.u, bf16[768,3456]{1,0:T(8,128)(2,1)} %bitcast.51, bf16[1536,768]{1,0:T(8,128)(2,1)} %bitcast.55, f32[1,768]{1,0:T(1,128)} %slice.137.rest_0_, ...), custom_call_target="tpu_custom_call" | custom-call | tf_op jit(solution)/shard_map/pallas_call | solution.py:566
  132.8 24.5 %all-gather.19.cloned.1.call-done = bf16[1,1536,768]{2,1,0:T(8,128)(2,1)} async-done(((bf16[1,96,768]{2,1,0:T(8,128)(2,1)}), bf16[1,1536,768]{2,1,0:T(8,128)(2,1)}) %all-gather.19.cloned.1.call-update) | async-done | bytes 2359312 | tf_op jit(solution)/shard_map/all_gather | solution.py:666
  157.3 57.8 %all-gather.17.cloned.1.call-done = bf16[1,768,3456]{2,1,0:T(8,128)(2,1)} async-done(((bf16[1,48,3456]{2,1,0:T(8,128)(2,1)}), bf16[1,768,3456]{2,1,0:T(8,128)(2,1)}) %all-gather.17.cloned.1.call-update) | async-done | bytes 5308432 | tf_op jit(solution)/shard_map/all_gather | solution.py:665
  215.1 18.8 %shard_map.238 = (f32[256,3456]{1,0:T(8,128)}, f32[256,1536]{1,0:T(8,128)}, f32[256,768]{1,0:T(8,128)}) custom-call(f32[2]{0:T(128)} %pad_maximum_fusion.2.flags, f32[256,768]{1,0:T(8,128)} %get-tuple-element.29.u, bf16[768,3456]{1,0:T(8,128)(2,1)} %bitcast.53, bf16[1536,768]{1,0:T(8,128)(2,1)} %bitcast.57, f32[1,768]{1,0:T(1,128)} %slice.153.rest_0_, ...), custom_call_target="tpu_custom_call" | custom-call | tf_op jit(solution)/shard_map/pallas_call | solution.py:566
  233.9 38.3 %shard_map.239 = (f32[256,768]{1,0:T(8,128)}, bf16[768,3456]{1,0:T(8,128)(2,1)}, bf16[1536,768]{1,0:T(8,128)(2,1)}, f32[8,1792]{1,0:T(8,128)}, f32[8,128]{1,0:T(8,128)}) custom-call(f32[2]{0:T(128)} %pad_maximum_fusion.2.flags, bf16[256,768]{1,0:T(8,128)(2,1)} %dynamic-slice_bitcast_fusion.g, f32[256,768]{1,0:T(8,128)} %get-tuple-element.29.u, ...), custom_call_target="tpu_custom_call" | custom-call | tf_op jit(solution)/shard_map/pallas_call | solution.py:599
  272.3 38.3 %shard_map.240 = (f32[256,768]{1,0:T(8,128)}, bf16[768,3456]{1,0:T(8,128)(2,1)}, bf16[1536,768]{1,0:T(8,128)(2,1)}, f32[8,1792]{1,0:T(8,128)}, f32[8,128]{1,0:T(8,128)}) custom-call(f32[2]{0:T(128)} %pad_maximum_fusion.2.flags, f32[256,768]{1,0:T(8,128)} %get-tuple-element.33.g, bf16[256,768]{1,0:T(8,128)(2,1)} %dynamic-slice_bitcast_fusion.1.u, ...), custom_call_target="tpu_custom_call" | custom-call | tf_op jit(solution)/shard_map/pallas_call | solution.py:599
  310.7 0.7 reduce-scatter.7.cloned.1.call-update
  311.5 0.7 reduce-scatter.5.cloned.1.call-update
  312.3 0.7 pad_maximum_fusion
  313.1 0.5 all-gather.21.cloned.1.call-update
  313.6 20.4 %reduce-scatter.11.cloned.1.call-done = bf16[96,768]{1,0:T(8,128)(2,1)} async-done(((bf16[1536,768]{1,0:T(8,128)(2,1)}), bf16[96,768]{1,0:T(8,128)(2,1)}) %reduce-scatter.11.cloned.1.call-update) | async-done | bytes 147472 | tf_op jit(solution)/shard_map/reduce_scatter | solution.py:692
  334.0 66.1 %reduce-scatter.9.cloned.1.call-done = bf16[96,768]{1,0:T(8,128)(2,1)} async-done(((bf16[1536,768]{1,0:T(8,128)(2,1)}), bf16[96,768]{1,0:T(8,128)(2,1)}) %reduce-scatter.9.cloned.1.call-update) | async-done | bytes 147472 | tf_op jit(solution)/shard_map/reduce_scatter | solution.py:692
  400.1 1.8 maximum_convert_fusion.1
  402.0 80.8 %reduce-scatter.7.cloned.1.call-done = bf16[48,3456]{1,0:T(8,128)(2,1)} async-done(((bf16[768,3456]{1,0:T(8,128)(2,1)}), bf16[48,3456]{1,0:T(8,128)(2,1)}) %reduce-scatter.7.cloned.1.call-update) | async-done | bytes 331792 | tf_op jit(solution)/shard_map/reduce_scatter | solution.py:691
  482.8 83.0 %reduce-scatter.5.cloned.1.call-done = bf16[48,3456]{1,0:T(8,128)(2,1)} async-done(((bf16[768,3456]{1,0:T(8,128)(2,1)}), bf16[48,3456]{1,0:T(8,128)(2,1)}) %reduce-scatter.5.cloned.1.call-update) | async-done | bytes 331792 | tf_op jit(solution)/shard_map/reduce_scatter | solution.py:691
  565.8 2.3 maximum_convert_fusion
  568.2 9.9 %all-gather.5 = bf16[512,768]{1,0:T(8,128)(2,1)S(1)} all-gather(bf16[256,768]{1,0:T(8,128)(2,1)S(1)} %convert_element_type.34), channel_id=7, replica_groups=mesh['dir'=2,'dp'=16] {'dir'}, dimensions={0}, use_global_device_ids=true | all-gather | bytes 1179648 | tf_op jit(solution)/shard_map/all_gather | solution.py:682
  578.0 39.6 %psum.30 = f32[2,8,128]{2,1,0:T(8,128)S(1)} all-reduce(f32[2,8,128]{2,1,0:T(8,128)S(1)} %pad_maximum_fusion.1), channel_id=1, replica_groups=mesh['dir'=2,'dp'=16] {'dir','dp'}, use_global_device_ids=true, to_apply=%region_6.7 | all-reduce | flops 2048 | bytes 16384 | tf_op jit(solution)/shard_map/psum | solution.py:697
  617.6 0.6 slice.194
  618.2 0.6 fusion.15
  618.8 72.5 %all-reduce.12.cloned.1.call-done = f32[2,8,1792]{2,1,0:T(8,128)} async-done(((f32[2,8,1792]{2,1,0:T(8,128)}), f32[2,8,1792]{2,1,0:T(8,128)}) %all-reduce.12.cloned.1.call-update) | async-done | bytes 114704 | tf_op jit(solution)/shard_map/psum | solution.py:697
  691.4 0.8 slice.188
  692.2 0.9 slice.192
  693.1 0.9 slice.193
  694.0 0.9 slice.198
  694.9 0.6 constant_dynamic-slice_fusion.3
  695.5 0.6 constant_dynamic-slice_fusion.1
  696.2 0.6 constant_dynamic-slice_fusion
  696.8 0.7 constant_dynamic-slice_fusion.2
  697.5 23.8 %all-gather.21.cloned.1.call-done = f32[512,768]{1,0:T(8,128)} async-done(((f32[256,768]{1,0:T(8,128)}), f32[512,768]{1,0:T(8,128)}) %all-gather.21.cloned.1.call-update) | async-done | bytes 1572880 | tf_op jit(solution)/shard_map/all_gather | solution.py:694
  721.3 62.7 %all-reduce.14.cloned.1.call-done = (f32[2,48,3456]{2,1,0:T(8,128)}, f32[2,96,768]{2,1,0:T(8,128)}) async-done(((f32[2,48,3456]{2,1,0:T(8,128)}, f32[2,96,768]{2,1,0:T(8,128)}), (f32[2,48,3456]{2,1,0:T(8,128)}, f32[2,96,768]{2,1,0:T(8,128)})) %all-reduce.14.cloned.1.call-update) | async-done | bytes 1916944 | tf_op jit(solution)/shard_map/psum | solution.py:695
  784.0 1.9 slice.189
  785.9 2.1 slice.190
  788.0 1.4 slice.191
  789.5 0.9 copy.34
  790.3 1.1 copy.35
  791.5 0.3 copy-done.3
  791.8 0.8 copy.36
  (70 shorter events, 1.2 us)
Async XLA Ops:
  7.2 40.2 %copy-start = (bf16[2,256,768]{2,1,0:T(8,128)(2,1)S(1)}, bf16[2,256,768]{2,1,0:T(8,128)(2,1)}, u32[]{:S(2)}) copy-start(bf16[2,256,768]{2,1,0:T(8,128)(2,1)} %param.14) | copy-start | bytes 2359300
  7.2 48.9 %all-gather.15.cloned.1.call-start = ((), (), s32[]{:S(2)}) async-start(), calls=%async_computation.10 | async-start | bytes 2506752 | tf_op jit(solution)/shard_map/all_gather | solution.py:666
  9.0 3.6 copy-start.16
  9.1 6.9 copy-start.9
  9.1 6.9 copy-start.13
  9.1 6.9 copy-start.14
  9.1 6.9 copy-start.15
  9.1 105.0 %all-gather.13.cloned.1.call-start = ((), (), s32[]{:S(2)}) async-start(), calls=%async_computation.9 | async-start | bytes 5640192 | tf_op jit(solution)/shard_map/all_gather | solution.py:665
  10.3 31.4 %copy-start.10 = (f32[2,24]{1,0:T(2,128)S(1)}, f32[2,24]{1,0:T(2,128)}, u32[]{:S(2)}) copy-start(f32[2,24]{1,0:T(2,128)} %param.24) | copy-start | bytes 580
  10.3 31.4 %copy-start.11 = (f32[2,24]{1,0:T(2,128)S(1)}, f32[2,24]{1,0:T(2,128)}, u32[]{:S(2)}) copy-start(f32[2,24]{1,0:T(2,128)} %param.25) | copy-start | bytes 580
  11.2 36.9 %copy-start.4 = (bf16[2,256,768]{2,1,0:T(8,128)(2,1)S(1)}, bf16[2,256,768]{2,1,0:T(8,128)(2,1)}, u32[]{:S(2)}) copy-start(bf16[2,256,768]{2,1,0:T(8,128)(2,1)} %param.15) | copy-start | bytes 2359300
  11.2 146.1 %all-gather.19.cloned.1.call-start = ((), (), s32[]{:S(2)}) async-start(), calls=%async_computation.12 | async-start | bytes 2506752 | tf_op jit(solution)/shard_map/all_gather | solution.py:666
  12.0 36.9 %copy-start.12 = (f32[2,48]{1,0:T(2,128)S(1)}, f32[2,48]{1,0:T(2,128)}, u32[]{:S(2)}) copy-start(f32[2,48]{1,0:T(2,128)} %param.23) | copy-start | bytes 1156
  12.0 203.1 %all-gather.17.cloned.1.call-start = ((), (), s32[]{:S(2)}) async-start(), calls=%async_computation.11 | async-start | bytes 5640192 | tf_op jit(solution)/shard_map/all_gather | solution.py:665
  12.5 321.5 %reduce-scatter.11.cloned.1.call-start = ((), (), s32[]{:S(2)}) async-start(), calls=%async_computation.8 | async-start | bytes 2506752 | tf_op jit(solution)/shard_map/reduce_scatter | solution.py:692
  272.3 127.8 %reduce-scatter.9.cloned.1.call-start = ((), (), s32[]{:S(2)}) async-start(), calls=%async_computation.7 | async-start | bytes 2506752 | tf_op jit(solution)/shard_map/reduce_scatter | solution.py:692
  310.7 172.1 %reduce-scatter.7.cloned.1.call-start = ((), (), s32[]{:S(2)}) async-start(), calls=%async_computation.6 | async-start | bytes 5640192 | tf_op jit(solution)/shard_map/reduce_scatter | solution.py:691
  311.4 254.3 %reduce-scatter.5.cloned.1.call-start = ((), (), s32[]{:S(2)}) async-start(), calls=%async_computation.5 | async-start | bytes 5640192 | tf_op jit(solution)/shard_map/reduce_scatter | solution.py:691
  311.5 0.8 copy-start.5
  311.5 0.8 copy-start.6
  312.2 379.2 %all-reduce.12.cloned.1.call-start = ((), (), s32[]{:S(2)}) async-start(), calls=%async_computation.4 | async-start | bytes 229376 | tf_op jit(solution)/shard_map/psum | solution.py:697
  313.0 408.3 %all-gather.21.cloned.1.call-start = ((), (), s32[]{:S(2)}) async-start(), calls=%async_computation.13 | async-start | bytes 2359296 | tf_op jit(solution)/shard_map/all_gather | solution.py:694
  313.6 470.4 %all-reduce.14.cloned.1.call-start = ((), (), s32[]{:S(2)}) async-start(), calls=%async_computation.14 | async-start | bytes 3833856 | tf_op jit(solution)/shard_map/psum | solution.py:695
  565.8 2.4 copy-start.2
  568.1 9.9 %copy-start.7 = (f32[8,128]{1,0:T(8,128)S(1)}, f32[8,128]{1,0:T(8,128)}, u32[]{:S(2)}) copy-start(f32[8,128]{1,0:T(8,128)} %get-tuple-element.42) | copy-start | bytes 12292
  568.1 9.9 %copy-start.8 = (f32[8,128]{1,0:T(8,128)S(1)}, f32[8,128]{1,0:T(8,128)}, u32[]{:S(2)}) copy-start(f32[8,128]{1,0:T(8,128)} %get-tuple-element.41) | copy-start | bytes 12292
  785.9 4.4 copy-start.1
  790.3 1.5 copy-start.3
Sparse Core Ops, SparseCore 0:
  10.9 45.2 all-gather.14
  58.9 55.1 all-gather.12
  116.3 40.9 all-gather.18
  159.9 55.1 all-gather.16
  272.4 61.5 reduce-scatter.10
  338.1 61.9 reduce-scatter.8
  404.1 78.6 reduce-scatter.6
  486.8 78.8 reduce-scatter.4
  571.9 119.4 all-reduce.11
  693.3 27.9 all-gather.20
  724.8 59.1 all-reduce.13
